TPU v7x, 128 devices: a whole 4x4x4 slice. The times are simulated.
128 devices in a mesh: chan: 8 (over x, core), row: 16 (over z, y).
Axes of the slice: x: 4, y: 4, z: 4, core: 2. Of those that a mesh axis runs over, the one named last changes fastest.
Arguments:
- voltages: bfloat16 [8, 16, 2, 32768], P(None, None, None, 'chan'), may hold values from -6 to 6
- kernel: float32 [8, 4, 4], P('chan'), may hold values from 0.25 to 1.5
- route_lists: int32 [8, 16, 512], P(None, 'row'), may hold values from 0 to 4095, as said below
- row_members: int32 [1024, 64], P('row'), may hold values from 0 to 4095, as said below
- row_counts: int32 [1024], P('row'), may hold values from 0 to 64, as said below
- anchor_cols: int32 [1024, 64], P('row'), may hold values from 0 to 1023, as said below
Outputs:
- sky: float32 [8, 1024, 1024], P('chan', None, 'row')
Inputs may be any that keep to these rules, and one draw needn't show every extreme that they name: `route_lists`: in each group and slab the listed entries name dipoles of the group; the entries that some row_members entry below its count points to are distinct dipoles, and no dipole is pointed to from two slabs. In every draw one slab is named in all 512 slots of every group's list and gridded from all of them; the other slabs use fewer. `row_members`: entries below the row's count are slots of the row's slab, distinct over the whole slab; entries at and after the count name other slots of the same slab. `row_counts`: in every draw all 64 rows of one slab hold 64 dipoles. `anchor_cols`: the 64 columns of one row are distinct; kernel cells past the last column fall outside the grid.
All inputs are finite; a program needn't handle non-finite values.
Results may differ from a plain program's by a relative error of at most 0.0015.
Values may be sent and summed in bfloat16 or wider, within the bound.
No kernel may reach another device: no remote copies, remote signals or barrier semaphores. Data moves between devices by JAX's collectives and lax.ppermute only.
A program may use at most 128 MiB of HBM per device.

v0:
```python
import math

import jax
import jax.numpy as jnp
from jax import lax
from jax.sharding import PartitionSpec as P

NGRID = 1024
KERNEL_SIDE = 4


def passed_along(block, axis, distance):
    devices = range(lax.axis_size(axis))
    route = [(i - distance, i) for i in devices if i - distance in devices]
    return lax.ppermute(block, axis, route)


def twiddle_tables(length):
    product = (
        jnp.arange(length, dtype=jnp.int32)[:, None]
        * jnp.arange(length, dtype=jnp.int32)[None, :]
        % length
    )
    angles = product.astype(jnp.float32) * (-2.0 * math.pi / length)
    return (jnp.cos(angles).astype(jnp.bfloat16), jnp.sin(angles).astype(jnp.bfloat16))


def per_device(voltages, kernel, route_lists, row_members, row_counts, anchor_cols):
    chan_count = lax.axis_size("chan")
    group_size = voltages.shape[3]
    samples = voltages.shape[1]
    slab_rows = row_members.shape[0]
    row_slots = row_members.shape[1]
    block_rows = math.gcd(slab_rows, 16)
    block_count = slab_rows // block_rows
    member_blocks = row_members.reshape(block_count, block_rows, row_slots)
    count_blocks = row_counts.reshape(block_count, block_rows)
    column_blocks = anchor_cols.reshape(block_count, block_rows, row_slots)
    grid_columns = jnp.arange(NGRID, dtype=jnp.int32)
    slot_index = jnp.arange(row_slots, dtype=jnp.int32)
    twiddle_cos, twiddle_sin = twiddle_tables(NGRID)
    group_offsets = jnp.arange(chan_count, dtype=jnp.int32)[:, None] * group_size
    global_ids = (route_lists[:, 0, :] + group_offsets).reshape(-1)
    received = jnp.take(
        lax.all_to_all(voltages, "chan", split_axis=0, concat_axis=3, tiled=True),
        global_ids,
        axis=3,
    )
    samples_here = received.shape[1]
    received_flat = received[0]

    def grid_block(block_inputs):
        members, counts, columns = block_inputs
        chosen = jnp.take(received_flat, members, axis=2)
        is_live = slot_index[None, :] < counts[:, None]
        onehot = (
            (columns[:, :, None] == grid_columns[None, None, :]) & is_live[:, :, None]
        ).astype(jnp.bfloat16)
        return jnp.einsum(
            "tcbp,bpx->tcbx", chosen, onehot, preferred_element_type=jnp.float32
        ).astype(jnp.bfloat16)

    blocks = lax.map(grid_block, (member_blocks, count_blocks, column_blocks))
    anchored = jnp.moveaxis(blocks, 0, 2).reshape(samples_here, 2, slab_rows, NGRID)
    upper_rim = passed_along(anchored[:, :, slab_rows - (KERNEL_SIDE - 1) :, :], "row", 1)
    extended = jnp.concatenate([upper_rim, anchored], axis=2).astype(jnp.float32)
    extended = jnp.pad(extended, ((0, 0), (0, 0), (0, 0), (KERNEL_SIDE - 1, 0)))
    kernel_taps = kernel[0]
    aperture = jnp.zeros((samples, 2, slab_rows, NGRID), jnp.float32)
    for tap_row in range(KERNEL_SIDE):
        for tap_col in range(KERNEL_SIDE):
            window = extended[
                :,
                :,
                KERNEL_SIDE - 1 - tap_row : KERNEL_SIDE - 1 - tap_row + slab_rows,
                KERNEL_SIDE - 1 - tap_col : KERNEL_SIDE - 1 - tap_col + NGRID,
            ]
            aperture = aperture + kernel_taps[tap_row, tap_col] * window
    aperture = aperture.astype(jnp.bfloat16)
    ap_real = aperture[:, 0]
    ap_imag = aperture[:, 1]
    spec_real = jnp.einsum(
        "tyx,xu->tyu", ap_real, twiddle_cos, preferred_element_type=jnp.float32
    ) - jnp.einsum("tyx,xu->tyu", ap_imag, twiddle_sin, preferred_element_type=jnp.float32)
    spec_imag = jnp.einsum(
        "tyx,xu->tyu", ap_real, twiddle_sin, preferred_element_type=jnp.float32
    ) + jnp.einsum("tyx,xu->tyu", ap_imag, twiddle_cos, preferred_element_type=jnp.float32)
    packed = jnp.stack((spec_real, spec_imag), axis=1).astype(jnp.bfloat16)
    slab_block = lax.all_to_all(packed, "row", split_axis=3, concat_axis=2, tiled=True)
    part_real = slab_block[:, 0]
    part_imag = slab_block[:, 1]
    image_real = jnp.einsum(
        "yw,tym->twm", twiddle_cos, part_real, preferred_element_type=jnp.float32
    ) - jnp.einsum("yw,tym->twm", twiddle_sin, part_imag, preferred_element_type=jnp.float32)
    image_imag = jnp.einsum(
        "yw,tym->twm", twiddle_sin, part_real, preferred_element_type=jnp.float32
    ) + jnp.einsum("yw,tym->twm", twiddle_cos, part_imag, preferred_element_type=jnp.float32)
    power_terms = image_real * image_real + image_imag * image_imag
    scale_factor = 1.0 / (group_size * chan_count * samples * KERNEL_SIDE * KERNEL_SIDE)
    sky_image = jnp.sum(power_terms, axis=0) * scale_factor
    return sky_image[None]


def solution(mesh):
    in_specs = (
        P(None, None, None, "chan"),
        P("chan", None, None),
        P(None, "row", None),
        P("row", None),
        P("row"),
        P("row", None),
    )
    out_specs = P("chan", None, "row")
    return jax.shard_map(
        per_device, mesh=mesh, in_specs=in_specs, out_specs=out_specs, check_vma=False
    )
```

profile of v0, /device:TPU:0, one launch (start us, length us, event | category | flops | bytes accessed | tf_op | source)
XLA Modules:
  0.0 452.4 jit_solution(15107161584241665445)
XLA Ops:
  0.0 0.0 copy-start.4
  0.0 0.0 copy-start.2
  0.0 4.5 all-to-all-start
  4.5 0.1 broadcast_bitcast_fusion.1
  4.6 0.0 copy-done.4
  4.6 0.1 reshape.135
  4.7 0.0 copy-done.2
  4.8 26.9 %all-to-all-done = bf16[8,16,2,4096]{3,2,1,0:T(2,128)(2,1)S(1)} async-done(((bf16[8,16,2,4096]{3,2,1,0:T(2,128)(2,1)}), bf16[8,16,2,4096]{3,2,1,0:T(2,128)(2,1)S(1)}, u32[]{:S(2)}, u32[]{:S(2)}) %all-to-all-start) | async-done | bytes 2097184 | tf_op jit(solution)/shard_map/all_to_all | solution.py:45
  31.7 27.1 %copy.22 = bf16[1,16,2,8,4096]{1,2,4,3,0:T(2,128)(2,1)} copy(bf16[1,16,2,8,4096]{4,2,1,3,0:T(2,128)(2,1)S(1)} %bitcast.150) | data formatting | bytes 4194304 | tf_op jit(solution)/shard_map/all_to_all | solution.py:45
  58.8 0.0 copy-start.1
  58.8 32.7 %gather_fusion.1 = bf16[4096,16,2]{1,2,0:T(2,128)(2,1)} fusion(bf16[16,2,32768]{0,1,2:T(2,128)(2,1)} %bitcast.149, s32[4096]{0:T(1024)S(1)} %broadcast_clamp_fusion.1), kind=kCustom, calls=%fused_computation.1 | custom fusion | bytes 540672 | tf_op jit(solution)/shard_map/jit(_take)/gather | solution.py:44
  91.5 15.5 %fusion.79 = bf16[16,2,4096]{0,1,2:T(2,128)(2,1)S(1)} fusion(bf16[4096,16,2]{1,2,0:T(2,128)(2,1)} %gather_fusion.1, pred[4096]{0:T(1024)(128)(4,1)S(1)} %compare_and_fusion.1), kind=kLoop, calls=%fused_computation.104 | loop fusion | flops 131072 | bytes 528384 | tf_op jit(solution)/shard_map/jit(_take)/select_n | solution.py:44
  107.0 0.0 copy-done.1
  107.0 27.7 %while.11 = (s32[]{:T(128)}, bf16[4,16,2,16,1024]{4,1,2,3,0:T(8,128)(2,1)}, s32[4,16,64]{2,1,0:T(8,128)}, s32[4,16]{1,0:T(4,128)S(1)}, s32[4,16,64]{2,1,0:T(8,12...) while((s32[]{:T(128)}, bf16[4,16,2,16,1024]{4,1,2,3,0:T(8,128)(2,1)}, ...), condition=%wide.region_1.2_spmd.clone, body=%wide.region_0.1_spmd.clone.sunk | while | flops 69774336 | bytes 1426205 | solution.py:63
  107.1 0.1 iota_compare_fusion.3
  107.1 0.1 reshape.173
  107.2 3.7 gather_fusion
  110.9 0.3 copy.29
  111.3 0.7 dynamic-slice_bitcast_fusion.2
  112.0 2.0 fusion.126
  114.0 0.1 iota_compare_fusion.3
  114.0 0.1 reshape.173
  114.1 3.7 gather_fusion
  117.8 0.3 copy.29
  118.2 0.7 dynamic-slice_bitcast_fusion.2
  118.9 2.0 fusion.126
  120.9 0.1 iota_compare_fusion.3
  121.0 0.1 reshape.173
  121.0 3.7 gather_fusion
  124.7 0.3 copy.29
  125.1 0.7 dynamic-slice_bitcast_fusion.2
  125.8 2.0 fusion.126
  127.8 0.1 iota_compare_fusion.3
  127.9 0.1 reshape.173
  128.0 3.7 gather_fusion
  131.7 0.3 copy.29
  132.0 0.7 dynamic-slice_bitcast_fusion.2
  132.7 2.0 fusion.126
  134.7 4.5 copy.18
  139.2 0.1 slice.156
  139.4 3.5 collective-permute-start
  142.9 0.0 copy-done.3
  142.9 0.7 fusion.118
  143.6 4.6 %collective-permute-done = bf16[16,2,3,1024]{3,2,0,1:T(4,128)(2,1)S(1)} collective-permute-done((bf16[16,2,3,1024]{3,2,0,1:T(4,128)(2,1)S(1)}, bf16[16,2,3,1024]{3,2,0,1:T(4,128)(2,1)S(1)}, u32[]{:S(2)}, u32[]{:S(2)}) %collective-permute-start) | collective-permute-done | bytes 196640 | tf_op jit(solution)/shard_map/ppermute | solution.py:15
  148.2 1.5 maximum_convert_fusion
  149.7 36.7 %fusion.52 = bf16[16,2,64,1024]{3,2,0,1:T(8,128)(2,1)S(1)} fusion(f32[16,2,67,1024]{3,2,0,1:T(8,128)S(1)} %maximum_convert_fusion, f32[]{:T(128)} %bitcast.27, f32[]{:T(128)} %bitcast.26, f32[]{:T(128)} %bitcast.25, f32[]{:T(128)} %bitcast.24, f32[]{:T(128)} %bitcast.23, f32[]{:T(128)} %bitcast.22, f32[]{:T(128)} %bitcast.21, f32[]{:T(128)} %bitcast.20, ...), kind=kLoop, calls=%fused_computation.70 | loop fusion | flops 67108864 | bytes 47185984 | tf_op jit(solution)/shard_map/convert_element_type | solution.py:79
  186.4 16.8 %fusion.69 = f32[16,64,1024]{2,1,0:T(8,128)S(1)} fusion(bf16[16,2,64,1024]{3,2,0,1:T(8,128)(2,1)S(1)} %fusion.52), kind=kOutput, calls=%fused_computation.99 | convolution fusion | flops 2163212288 | bytes 6291456 | tf_op jit(solution)/shard_map/tyx,xu->tyu/dot_general | solution.py:84
  203.2 16.8 %fusion.75 = f32[16,64,1024]{2,1,0:T(8,128)S(1)} fusion(bf16[16,2,64,1024]{3,2,0,1:T(8,128)(2,1)S(1)} %fusion.52), kind=kOutput, calls=%fused_computation.102 | convolution fusion | flops 2163212288 | bytes 6291456 | tf_op jit(solution)/shard_map/tyx,xu->tyu/dot_general | solution.py:87
  220.0 17.2 %fusion.61 = bf16[16,1,64,1024]{3,2,0,1:T(8,128)(2,1)S(1)} fusion(f32[16,64,1024]{2,1,0:T(8,128)S(1)} %fusion.69, bf16[16,2,64,1024]{3,2,0,1:T(8,128)(2,1)S(1)} %fusion.52), kind=kOutput, calls=%fused_computation.90 | convolution fusion | flops 2165309440 | bytes 8388608 | tf_op jit(solution)/shard_map/tyx,xu->tyu/dot_general | solution.py:82
  237.1 17.3 %fusion.62 = bf16[16,1,64,1024]{3,2,0,1:T(8,128)(2,1)S(1)} fusion(f32[16,64,1024]{2,1,0:T(8,128)S(1)} %fusion.75, bf16[16,2,64,1024]{3,2,0,1:T(8,128)(2,1)S(1)} %fusion.52), kind=kOutput, calls=%fused_computation.91 | convolution fusion | flops 2165309440 | bytes 8388608 | tf_op jit(solution)/shard_map/tyx,xu->tyu/dot_general | solution.py:85
  254.5 2.3 pad_maximum_fusion
  256.8 12.9 %copy.19 = bf16[16,2,64,1024]{2,0,1,3:T(8,128)(2,1)} copy(bf16[16,2,64,1024]{3,2,0,1:T(8,128)(2,1)} %pad_maximum_fusion) | data formatting | bytes 8388608 | tf_op jit(solution)/shard_map/stack | solution.py:88
  269.8 14.0 %reshape.166 = bf16[16,2,65536]{2,1,0:T(2,128)(2,1)} reshape(bf16[1024,2,16,64]{3,2,1,0:T(8,128)(2,1)} %bitcast.143) | data formatting | bytes 8388608
  283.8 60.3 %all_to_all.36 = bf16[16,2,65536]{2,1,0:T(2,128)(2,1)} all-to-all(bf16[16,2,65536]{2,1,0:T(2,128)(2,1)} %reshape.166), channel_id=1, replica_groups=mesh['chan'=8,'row'=16] {'row'}, dimensions={0} | all-to-all | bytes 8388608 | tf_op jit(solution)/shard_map/all_to_all | solution.py:89
  344.0 13.7 %reshape.167 = bf16[1024,2,16,64]{3,2,1,0:T(8,128)(2,1)} reshape(bf16[16,2,65536]{2,1,0:T(2,128)(2,1)} %all_to_all.36) | data formatting | bytes 8388608
  357.7 12.0 %copy.27 = bf16[16,2,64,16,64]{2,3,4,0,1:T(8,128)(2,1)} copy(bf16[16,2,64,16,64]{2,0,1,4,3:T(8,128)(2,1)} %bitcast.144) | data formatting | bytes 8388608 | tf_op jit(solution)/shard_map/all_to_all | solution.py:89
  369.7 12.0 %all_to_all.33 = bf16[16,2,1024,64]{2,3,0,1:T(8,128)(2,1)} reshape(bf16[16,2,16,64,64]{3,2,4,0,1:T(8,128)(2,1)} %bitcast.145) | data formatting | bytes 8388608 | tf_op jit(solution)/shard_map/all_to_all | solution.py:89
  381.7 0.0 copy-start
  381.8 18.5 %fusion.63 = f32[16,64,1024]{2,1,0:T(8,128)S(1)} fusion(bf16[16,2,1024,64]{2,3,0,1:T(8,128)(2,1)} %all_to_all.33), kind=kOutput, calls=%fused_computation.96 | convolution fusion | flops 2163212288 | bytes 6291456 | tf_op jit(solution)/shard_map/yw,tym->twm/dot_general | solution.py:95
  400.3 0.0 copy-done
  400.3 17.0 %fusion.65 = f32[16,64,1024]{2,1,0:T(8,128)S(1)} fusion(bf16[16,2,1024,64]{2,3,0,1:T(8,128)(2,1)S(1)} %copy-done), kind=kOutput, calls=%fused_computation.97 | convolution fusion | flops 2163212288 | bytes 6291456 | tf_op jit(solution)/shard_map/yw,tym->twm/dot_general | solution.py:94
  417.3 16.7 %fusion.71 = f32[16,64,1024]{2,1,0:T(8,128)S(1)} fusion(bf16[16,2,1024,64]{2,3,0,1:T(8,128)(2,1)S(1)} %copy-done), kind=kOutput, calls=%fused_computation.100 | convolution fusion | flops 2163212288 | bytes 6291456 | tf_op jit(solution)/shard_map/yw,tym->twm/dot_general | solution.py:97
  434.1 17.4 %add_reduce_fusion = f32[64,1024]{1,0:T(8,128)S(1)} fusion(f32[16,64,1024]{2,1,0:T(8,128)S(1)} %fusion.63, f32[16,64,1024]{2,1,0:T(8,128)S(1)} %fusion.71, f32[16,64,1024]{2,1,0:T(8,128)S(1)} %fusion.65, bf16[16,2,1024,64]{2,3,0,1:T(8,128)(2,1)S(1)} %copy-done), kind=kOutput, calls=%fused_computation.79 | convolution fusion | flops 2169438208 | bytes 14942208 | tf_op jit(solution)/shard_map/yw,tym->twm/dot_general | solution.py:92
  451.5 0.7 multiply_bitcast_fusion
  (20 shorter events, 0.1 us)
Async XLA Ops:
  0.0 4.6 %copy-start.4 = (s32[64]{0:T(128)S(1)}, s32[64]{0:T(128)}, u32[]{:S(2)}) copy-start(s32[64]{0:T(128)} %param.12) | copy-start | bytes 772
  0.0 4.7 %copy-start.2 = (s32[8,1,512]{2,1,0:T(1,128)S(1)}, s32[8,1,512]{2,1,0:T(1,128)}, u32[]{:S(2)}) copy-start(s32[8,1,512]{2,1,0:T(1,128)} %param.10) | copy-start | bytes 49156
  0.0 31.7 %all-to-all-start = ((bf16[8,16,2,4096]{3,2,1,0:T(2,128)(2,1)}), bf16[8,16,2,4096]{3,2,1,0:T(2,128)(2,1)S(1)}, u32[]{:S(2)}, u32[]{:S(2)}) async-start(bf16[8,16,2,4096]{3,2,1,0:T(2,128)(2,1)} %param.8), calls=%async_computation | async-start | bytes 4194304 | tf_op jit(solution)/shard_map/all_to_all | solution.py:45
  58.8 48.2 %copy-start.1 = (s32[64,64]{1,0:T(8,128)S(1)}, s32[64,64]{1,0:T(8,128)}, u32[]{:S(2)}) copy-start(s32[64,64]{1,0:T(8,128)} %param.11) | copy-start | bytes 49156
  134.7 8.2 %copy-start.3 = (f32[1,4,4]{2,1,0:T(4,128)S(1)}, f32[1,4,4]{2,1,0:T(4,128)}, u32[]{:S(2)}) copy-start(f32[1,4,4]{2,1,0:T(4,128)} %param.9) | copy-start | bytes 196
  139.4 8.8 %collective-permute-start = (bf16[16,2,3,1024]{3,2,0,1:T(4,128)(2,1)S(1)}, bf16[16,2,3,1024]{3,2,0,1:T(4,128)(2,1)S(1)}, u32[]{:S(2)}, u32[]{:S(2)}) collective-permute-start(bf16[16,2,3,1024]{3,2,0,1:T(4,128)(2,1)S(1)} %slice.156), channel_id=1, source_target_pairs={{0,1},{1,2},{2,3},{3,4},{4,5},{5,6},{6,7},{7,8},{8,9},{9,10},{10,1... | collective-permute-start | bytes 589832 | tf_op jit(solution)/shard_map/ppermute | solution.py:15
  381.7 18.6 %copy-start = (bf16[16,2,1024,64]{2,3,0,1:T(8,128)(2,1)S(1)}, bf16[16,2,1024,64]{2,3,0,1:T(8,128)(2,1)}, u32[]{:S(2)}) copy-start(bf16[16,2,1024,64]{2,3,0,1:T(8,128)(2,1)} %all_to_all.33) | copy-start | bytes 12582916
where the time goes:
time: 462 us; the launch traced here: 452 us
  local copies, waits for them, and re-layouts  149 us (32%)
  matrix products  146 us (32%)
  blocking collectives  60.3 us (13%)
  other arithmetic  57.1 us (12%)
  waiting for transfers between devices  31.5 us (7%)
  starting transfers between devices  8.01 us (2%)
    all_to_all x1, blocking collectives, per_device(): lax.all_to_all(packed, 'row', split_axis=3, concat_axis=2, tiled=True)  60.3 us
    convert_element_type x1, other arithmetic, per_device(): aperture = aperture.astype(jnp.bfloat16)  36.7 us
    gather x1, local copies, waits for them, and re-layouts, per_device(): jnp.take(lax.all_to_all(voltages, 'chan', split_axis=0, concat_axis=3, ti...  32.7 us
    unnamed x15, local copies, waits for them, and re-layouts  27.8 us
    all_to_all x1, local copies, waits for them, and re-layouts, per_device(): lax.all_to_all(voltages, 'chan', split_axis=0, concat_axis=3, tiled=True)  27.1 us
    all_to_all x1, waiting for transfers between devices, per_device(): lax.all_to_all(voltages, 'chan', split_axis=0, concat_axis=3, tiled=True)  26.9 us
    all_to_all x2, local copies, waits for them, and re-layouts, per_device(): lax.all_to_all(packed, 'row', split_axis=3, concat_axis=2, tiled=True)  24 us
    dot_general x1, matrix products, per_device(): jnp.einsum('yw,tym->twm', twiddle_sin, part_real, preferred_element_type=...  18.5 us
  transfers between devices with their start and end apart: 2, of which 2 were waited for; matrix products, arithmetic and copies ran while one was open for 0% of the time, Pallas kernels for 0%

commit v1 on v0

v1 whole, which is shorter than its diff:
```python
import jax
import jax.numpy as jnp
import numpy as np
from jax import lax
from jax.experimental import pallas as pl
from jax.experimental.pallas import tpu as pltpu
from jax.sharding import PartitionSpec as P

NGRID = 1024
KERNEL_SIDE = 4
RADIX = 4
POINTS = NGRID // RADIX
LANES = 128
F32 = jnp.float32
BF16 = jnp.bfloat16


def stage_tables():
    n = np.arange(NGRID, dtype=np.int64)
    product = (n[:, None] * n[None, :POINTS]) % NGRID
    angles = product.astype(np.float32) * np.float32(-2.0 * np.pi / NGRID)
    cos = np.cos(angles).astype(np.float32)
    sin = np.sin(angles).astype(np.float32)
    parts = []
    for q in range(RADIX):
        c, s = cos[q::RADIX], sin[q::RADIX]
        parts.append(np.block([[c, s], [-s, c]]))
    table = np.stack(parts)
    return (
        np.ascontiguousarray(table.transpose(0, 2, 1)).astype(jnp.bfloat16),
        table.astype(jnp.bfloat16),
    )


def butterfly(re, im):
    ra, rb = re[0] + re[2], re[0] - re[2]
    rc, rd = re[1] + re[3], re[1] - re[3]
    ia, ib = im[0] + im[2], im[0] - im[2]
    ic, id_ = im[1] + im[3], im[1] - im[3]
    return (ra + rc, rb + id_, ra - rc, rb - id_), (ia + ic, ib - rd, ia - ic, ib + rd)


def lookup(rows_of, index, count):
    lane = index & (LANES - 1)
    row = index >> 7
    first = jnp.zeros(index.shape, F32)
    second = jnp.zeros(index.shape, F32)
    for k in range(count):
        a, b = rows_of(k)
        hit = row == k
        a = jnp.take_along_axis(a, lane, axis=1, mode="promise_in_bounds")
        b = jnp.take_along_axis(b, lane, axis=1, mode="promise_in_bounds")
        first = jnp.where(hit, a, first)
        second = jnp.where(hit, b, second)
    return first, second


def sample_kernel(
    taps, volts, lists, wide, tall, power, table, slots, dense, aperture, spectrum
):
    slabs = lists.shape[0]
    groups = volts.shape[0]
    slab_points = POINTS // slabs

    for g in range(groups):
        for i in range(2):
            table[i, :, g, :] = volts[g, i].astype(F32)
    for i in range(2):
        for qy in range(RADIX):
            for qx in range(RADIX):
                for w in range(2):
                    dense[i, qy, qx, w, 0:8, :] = jnp.zeros((8, LANES), F32)

    sub = lax.broadcasted_iota(jnp.int32, (8, LANES), 0)
    lane = lax.broadcasted_iota(jnp.int32, (8, LANES), 1)
    half = (lane >= 64).astype(jnp.int32)
    own_row = [sub == 2 * s + half for s in range(4)]
    cell = lax.broadcasted_iota(jnp.int32, (POINTS, 4 * LANES), 0).astype(BF16)

    def grid_slab(r, carry):
        routes = lists[r, 0].astype(jnp.int32)
        members = lists[r, 1].astype(jnp.int32)
        columns = lists[r, 2].astype(jnp.int32)

        def group_rows(k):
            return tuple(
                jnp.broadcast_to(table[i, k][None], (4, 8, LANES)).reshape(32, LANES)
                for i in range(2)
            )

        slot_re, slot_im = lookup(group_rows, routes, 32)
        slots[0] = slot_re
        slots[1] = slot_im

        def slot_rows(k):
            return tuple(
                jnp.broadcast_to(slots[i, k : k + 1, :], (32, LANES)) for i in range(2)
            )

        values = lookup(slot_rows, members, 32)
        phase = columns & (RADIX - 1)
        point = (columns >> 2).astype(F32)
        for qy in range(RADIX):
            part = slice(8 * qy, 8 * qy + 8)
            planes = [
                jnp.where(phase[part] == qx, values[i][part], 0.0)
                for qx in range(RADIX)
                for i in range(2)
            ]
            for h in range(2):
                left = jnp.concatenate(
                    [
                        jnp.concatenate(
                            [
                                jnp.where(
                                    own_row[s],
                                    jnp.broadcast_to(
                                        plane[4 * h + s : 4 * h + s + 1, :], (8, LANES)
                                    ),
                                    0.0,
                                )
                                for s in range(4)
                            ],
                            axis=1,
                        )
                        for plane in planes
                    ],
                    axis=0,
                ).astype(BF16)
                spot = jnp.concatenate(
                    [
                        point[8 * qy + 4 * h + s : 8 * qy + 4 * h + s + 1, :]
                        for s in range(4)
                    ],
                    axis=1,
                ).astype(BF16)
                onehot = jnp.where(cell == spot, BF16(1), BF16(0))
                placed = lax.dot_general(
                    left, onehot, (((1,), (1,)), ((), ())), preferred_element_type=F32
                )
                start = pl.multiple_of(8 + r * slab_points + 8 * h, 8)
                for qx in range(RADIX):
                    for i in range(2):
                        at = (qx * 2 + i) * 8
                        for w in range(2):
                            dense[i, qy, qx, w, pl.ds(start, 8), :] = placed[
                                at : at + 8, w * LANES : (w + 1) * LANES
                            ]
        return carry

    lax.fori_loop(0, slabs, grid_slab, 0)

    first_lane = lax.broadcasted_iota(jnp.int32, (16, POINTS), 1) == 0

    def convolve(t, carry):
        for i in range(2):
            for qy in range(RADIX):
                sums = [jnp.zeros((16, POINTS), F32) for _ in range(RADIX)]
                for ky in range(KERNEL_SIDE):
                    source = (qy - ky) % RADIX
                    start = 8 + 16 * t - (1 if ky > qy else 0)
                    here = [
                        jnp.concatenate(
                            [
                                dense[i, source, qx, w, pl.ds(start, 16), :]
                                for w in range(2)
                            ],
                            axis=1,
                        )
                        for qx in range(RADIX)
                    ]
                    before = [
                        None
                        if qx == 0
                        else jnp.where(first_lane, 0.0, pltpu.roll(here[qx], 1, 1))
                        for qx in range(RADIX)
                    ]
                    for qx in range(RADIX):
                        for kx in range(KERNEL_SIDE):
                            near = before if kx > qx else here
                            sums[qx] = (
                                sums[qx] + taps[ky, kx] * near[(qx - kx) % RADIX]
                            )
                row = pl.multiple_of(qy * POINTS + 16 * t, 16)
                for qx in range(RADIX):
                    at = (2 * qx + i) * POINTS
                    aperture[pl.ds(row, 16), at : at + POINTS] = sums[qx].astype(BF16)
        return carry

    lax.fori_loop(0, POINTS // 16, convolve, 0)

    def row_transform(qy, carry):
        rows = pl.ds(pl.multiple_of(qy * POINTS, POINTS), POINTS)
        parts = [
            lax.dot_general(
                wide[q],
                aperture[rows, 2 * q * POINTS : 2 * (q + 1) * POINTS],
                (((1,), (1,)), ((), ())),
                preferred_element_type=F32,
            )
            for q in range(RADIX)
        ]
        re, im = butterfly(
            [part[:POINTS] for part in parts], [part[POINTS:] for part in parts]
        )
        at = pl.multiple_of(qy * 2 * POINTS, 2 * POINTS)
        for m in range(RADIX):
            spectrum[m * POINTS : (m + 1) * POINTS, pl.ds(at, POINTS)] = re[m].astype(
                BF16
            )
            spectrum[
                m * POINTS : (m + 1) * POINTS, pl.ds(at + POINTS, POINTS)
            ] = im[m].astype(BF16)
        return carry

    lax.fori_loop(0, RADIX, row_transform, 0)

    def column_transform(n, carry):
        rows = pl.ds(pl.multiple_of(n * 128, 128), 128)
        parts = [
            jnp.dot(
                spectrum[rows, 2 * q * POINTS : 2 * (q + 1) * POINTS],
                tall[q],
                preferred_element_type=F32,
            )
            for q in range(RADIX)
        ]
        re, im = butterfly(
            [part[:, :POINTS] for part in parts], [part[:, POINTS:] for part in parts]
        )
        for m in range(RADIX):
            power[rows, m * POINTS : (m + 1) * POINTS] = (
                re[m] * re[m] + im[m] * im[m]
            ).astype(BF16)
        return carry

    lax.fori_loop(0, NGRID // 128, column_transform, 0)


def sample_power(taps, volts, lists, wide, tall, interpret=False):
    return pl.pallas_call(
        sample_kernel,
        out_shape=jax.ShapeDtypeStruct((NGRID, NGRID), BF16),
        in_specs=[pl.BlockSpec(memory_space=pltpu.SMEM)]
        + [pl.BlockSpec(memory_space=pltpu.VMEM)] * 4,
        out_specs=pl.BlockSpec(memory_space=pltpu.VMEM),
        scratch_shapes=[
            pltpu.VMEM((2, 32, 8, LANES), F32),
            pltpu.VMEM((2, 32, LANES), F32),
            pltpu.VMEM((2, RADIX, RADIX, 2, POINTS + 8, LANES), F32),
            pltpu.VMEM((NGRID, 2 * NGRID), BF16),
            pltpu.VMEM((NGRID, 2 * NGRID), BF16),
        ],
        compiler_params=pltpu.CompilerParams(vmem_limit_bytes=56 * 2**20),
        interpret=interpret,
    )(taps, volts, lists, wide, tall)


def slab_lists(route_lists, row_members, row_counts, anchor_cols):
    routes = route_lists[:, 0, :].reshape(8, 4, LANES).transpose(1, 0, 2)
    slot = ((row_members >> 7) & 3) * 1024 + (row_members >> 9) * LANES
    slot = slot + (row_members & (LANES - 1))
    live = jnp.arange(row_members.shape[1], dtype=jnp.int32)[None, :] < row_counts[:, None]
    slot = jnp.where(live, slot, -1)
    by_phase = [
        a.reshape(-1, RADIX, a.shape[1]).transpose(1, 0, 2).reshape(32, LANES)
        for a in (slot, anchor_cols)
    ]
    return jnp.stack([routes.reshape(32, LANES), *by_phase]).astype(jnp.int16)


def per_device(voltages, kernel, route_lists, row_members, row_counts, anchor_cols):
    chan_count = lax.axis_size("chan")
    row_count = lax.axis_size("row")
    group_size = voltages.shape[3]
    samples = voltages.shape[1]
    lists = slab_lists(route_lists, row_members, row_counts, anchor_cols)
    lists = jnp.broadcast_to(lists[None], (row_count,) + lists.shape)
    lists = lax.all_to_all(lists, "row", split_axis=0, concat_axis=0, tiled=True)
    mine = lax.dynamic_index_in_dim(voltages, lax.axis_index("row"), 1, keepdims=False)
    mine = mine.reshape(chan_count, 2, group_size // LANES, LANES)
    volts = lax.all_to_all(mine, "chan", split_axis=0, concat_axis=0, tiled=True)
    wide, tall = stage_tables()
    power = sample_power(kernel[0], volts, lists, jnp.asarray(wide), jnp.asarray(tall))
    power = power.reshape(row_count, NGRID // row_count, NGRID)
    power = lax.all_to_all(power, "row", split_axis=0, concat_axis=0, tiled=True)
    scale_factor = 1.0 / (group_size * chan_count * samples * KERNEL_SIDE * KERNEL_SIDE)
    sky_image = jnp.sum(power.astype(F32), axis=0) * scale_factor
    return sky_image.T[None]


def solution(mesh):
    in_specs = (
        P(None, None, None, "chan"),
        P("chan", None, None),
        P(None, "row", None),
        P("row", None),
        P("row"),
        P("row", None),
    )
    out_specs = P("chan", None, "row")
    return jax.shard_map(
        per_device, mesh=mesh, in_specs=in_specs, out_specs=out_specs, check_vma=False
    )
```

time: 462 us -> 111 us (0.24); the launches traced: 452 us -> 110 us
  local copies, waits for them, and re-layouts: 149 us -> 2.71 us
  matrix products: 146 us -> 0 us
  other arithmetic: 57.1 us -> 3.48 us
  Pallas kernels: 0 us -> 46.7 us
  waiting for transfers between devices: 31.5 us -> 3.55 us
  blocking collectives: 60.3 us -> 49.3 us
    dot_general x12 -> x0, matrix products: 146 us -> none  [the longest x1 18.5 us: per_device(): jnp.einsum('yw,tym->twm', twiddle_sin, part_real, preferred_element_type=...]
    all_to_all x3 -> x0, local copies, waits for them, and re-layouts: 51.1 us -> none  [the longest x1 27.1 us: per_device(): lax.all_to_all(voltages, 'chan', split_axis=0, concat_axis=3, tiled=True)]
    gather x9 -> x0, local copies, waits for them, and re-layouts: 48.8 us -> none  [the longest x1 32.7 us: per_device(): jnp.take(lax.all_to_all(voltages, 'chan', split_axis=0, concat_axis=3, ti...]
    pallas_call x0 -> x1, Pallas kernels: none -> 46.7 us  [sample_power(): pl.pallas_call(sample_kernel, out_shape=jax.ShapeDtypeStruct((NGRID, NGRI...]
    convert_element_type x2 -> x0, other arithmetic: 38.2 us -> none  [the longest x1 36.7 us: per_device(): aperture = aperture.astype(jnp.bfloat16)]
    unnamed x15 -> x4, local copies, waits for them, and re-layouts: 27.8 us -> 1.59 us
    all_to_all x1, waiting for transfers between devices: 26.9 us -> 3.55 us  [per_device(): lax.all_to_all(mine, 'chan', split_axis=0, concat_axis=0, tiled=True)]
    select_n x6 -> x0, other arithmetic: 15.6 us -> none  [the longest x2 15.5 us: per_device(): jnp.take(lax.all_to_all(voltages, 'chan', split_axis=0, concat_axis=3, ti...]
  transfers between devices with their start and end apart: 2 -> 1, of which waited for: 2 -> 1; matrix products, arithmetic and copies ran while one was open for 0% -> 2% of each run, Pallas kernels for 0% -> 0%
where the time goes in v1:
time: 111 us; the launch traced here: 110 us
  blocking collectives  49.3 us (44%)
  Pallas kernels  46.7 us (42%)
  starting transfers between devices  4.38 us (4%)
  waiting for transfers between devices  3.55 us (3%)
  other arithmetic  3.48 us (3%)
  local copies, waits for them, and re-layouts  2.71 us (2%)
    pallas_call x1, Pallas kernels, sample_power(): pl.pallas_call(sample_kernel, out_shape=jax.ShapeDtypeStruct((NGRID, NGRI...  46.7 us
    all_to_all x1, blocking collectives, per_device(): lax.all_to_all(power, 'row', split_axis=0, concat_axis=0, tiled=True)  31.5 us
    all_to_all x1, blocking collectives, per_device(): lax.all_to_all(lists, 'row', split_axis=0, concat_axis=0, tiled=True)  17.9 us
    all_to_all x1, starting transfers between devices, per_device(): lax.all_to_all(mine, 'chan', split_axis=0, concat_axis=0, tiled=True)  4.38 us
    all_to_all x1, waiting for transfers between devices, per_device(): lax.all_to_all(mine, 'chan', split_axis=0, concat_axis=0, tiled=True)  3.55 us
    another operation x3, other arithmetic  2.36 us
  transfers between devices with their start and end apart: 1, of which 1 were waited for; matrix products, arithmetic and copies ran while one was open for 2% of the time, Pallas kernels for 0%

profile of v1, /device:TPU:0, one launch (start us, length us, event | category | flops | bytes accessed | tf_op | source)
XLA Modules:
  0.0 110.2 jit_solution(14745004232881307058)
XLA Ops:
  0.0 0.0 copy-start
  0.0 1.6 %copy-done = bf16[8,16,2,4096]{3,2,1,0:T(2,128)(2,1)S(1)} copy-done((bf16[8,16,2,4096]{3,2,1,0:T(2,128)(2,1)S(1)}, bf16[8,16,2,4096]{3,2,1,0:T(2,128)(2,1)}, u32[]{:S(2)}) %copy-start) | copy-done | bytes 2097176
  1.6 0.1 constant_dynamic-slice_fusion
  1.7 0.8 reshape.44
  2.5 4.4 %all-to-all-start = ((bf16[8,2,32,128]{3,2,1,0:T(8,128)(2,1)}), bf16[8,2,32,128]{3,2,1,0:T(8,128)(2,1)S(1)}, u32[]{:S(2)}, u32[]{:S(2)}) async-start(bf16[8,2,32,128]{3,2,1,0:T(8,128)(2,1)} %reshape.44), calls=%async_computation | async-start | bytes 262144 | tf_op jit(solution)/shard_map/all_to_all | solution.py:282
  6.8 0.8 select_convert_fusion
  7.7 0.8 convert_reduce_fusion.1
  8.5 0.1 stack.10
  8.6 0.8 convert.20
  9.3 0.1 stack.11
  9.4 3.5 %all-to-all-done.volts = bf16[8,2,32,128]{3,2,1,0:T(8,128)(2,1)S(1)} async-done(((bf16[8,2,32,128]{3,2,1,0:T(8,128)(2,1)}), bf16[8,2,32,128]{3,2,1,0:T(8,128)(2,1)S(1)}, u32[]{:S(2)}, u32[]{:S(2)}) %all-to-all-start) | async-done | bytes 131104 | tf_op jit(solution)/shard_map/all_to_all | solution.py:282
  13.0 0.0 copy-start.1
  13.0 0.1 broadcast_in_dim.16
  13.0 17.9 %all_to_all.15.lists = s16[16,3,32,128]{3,2,1,0:T(8,128)(2,1)} all-to-all(s16[16,3,32,128]{3,2,1,0:T(8,128)(2,1)S(1)} %broadcast_in_dim.16), channel_id=1, replica_groups=mesh['chan'=8,'row'=16] {'row'}, dimensions={0} | all-to-all | bytes 786432 | tf_op jit(solution)/shard_map/all_to_all | solution.py:279
  30.9 0.0 copy-done.1
  30.9 46.7 %shard_map.82 = bf16[1024,1024]{1,0:T(8,128)(2,1)} custom-call(f32[4,4]{1,0:T(4,128)} %bitcast.21, bf16[8,2,32,128]{3,2,1,0:T(8,128)(2,1)} %copy-done.1, s16[16,3,32,128]{3,2,1,0:T(8,128)(2,1)} %all_to_all.15.lists, bf16[4,512,512]{2,1,0:T(8,128)(2,1)} %constant.32.clone.wide, bf16[4,512,512]{2,1,0:T(8,128)(2,1)} %constant.33.clone.tall), custom_call_target="tpu_custom_call" | custom-call | tf_op jit(solution)/shard_map/pallas_call | solution.py:241
  77.6 31.5 %all_to_all.16 = bf16[16,64,1024]{2,1,0:T(8,128)(2,1)S(1)} all-to-all(bf16[16,64,1024]{2,1,0:T(8,128)(2,1)} %bitcast.16), channel_id=1, replica_groups=mesh['chan'=8,'row'=16] {'row'}, dimensions={0} | all-to-all | bytes 4194304 | tf_op jit(solution)/shard_map/all_to_all | solution.py:286
  109.1 0.4 convert_reduce_fusion
  109.5 0.7 multiply_bitcast_fusion
  (5 shorter events, 0.0 us)
Async XLA Ops:
  0.0 1.6 %copy-start = (bf16[8,16,2,4096]{3,2,1,0:T(2,128)(2,1)S(1)}, bf16[8,16,2,4096]{3,2,1,0:T(2,128)(2,1)}, u32[]{:S(2)}) copy-start(bf16[8,16,2,4096]{3,2,1,0:T(2,128)(2,1)} %param.8) | copy-start | bytes 6291460
  2.5 10.5 %all-to-all-start = ((bf16[8,2,32,128]{3,2,1,0:T(8,128)(2,1)}), bf16[8,2,32,128]{3,2,1,0:T(8,128)(2,1)S(1)}, u32[]{:S(2)}, u32[]{:S(2)}) async-start(bf16[8,2,32,128]{3,2,1,0:T(8,128)(2,1)} %reshape.44), calls=%async_computation | async-start | bytes 262144 | tf_op jit(solution)/shard_map/all_to_all | solution.py:282
  13.0 17.9 %copy-start.1 = (bf16[8,2,32,128]{3,2,1,0:T(8,128)(2,1)}, bf16[8,2,32,128]{3,2,1,0:T(8,128)(2,1)S(1)}, u32[]{:S(2)}) copy-start(bf16[8,2,32,128]{3,2,1,0:T(8,128)(2,1)S(1)} %all-to-all-done.volts) | copy-start | bytes 393220

commit v2 on v1

--- a/solution.py
+++ b/solution.py
@@ -40,19 +40,8 @@
     return (ra + rc, rb + id_, ra - rc, rb - id_), (ia + ic, ib - rd, ia - ic, ib + rd)
 
 
-def lookup(rows_of, index, count):
-    lane = index & (LANES - 1)
-    row = index >> 7
-    first = jnp.zeros(index.shape, F32)
-    second = jnp.zeros(index.shape, F32)
-    for k in range(count):
-        a, b = rows_of(k)
-        hit = row == k
-        a = jnp.take_along_axis(a, lane, axis=1, mode="promise_in_bounds")
-        b = jnp.take_along_axis(b, lane, axis=1, mode="promise_in_bounds")
-        first = jnp.where(hit, a, first)
-        second = jnp.where(hit, b, second)
-    return first, second
+def pick(table_rows, index):
+    return jnp.take_along_axis(table_rows, index, axis=1, mode="promise_in_bounds")
 
 
 def sample_kernel(
@@ -73,53 +62,64 @@
 
     sub = lax.broadcasted_iota(jnp.int32, (8, LANES), 0)
     lane = lax.broadcasted_iota(jnp.int32, (8, LANES), 1)
-    half = (lane >= 64).astype(jnp.int32)
-    own_row = [sub == 2 * s + half for s in range(4)]
-    cell = lax.broadcasted_iota(jnp.int32, (POINTS, 4 * LANES), 0).astype(BF16)
-
-    def grid_slab(r, carry):
+    own_row = sub == lane >> 4
+
+    def grid_chunks(r, chunks, list_chunks):
+        size = 8 * chunks
         routes = lists[r, 0].astype(jnp.int32)
-        members = lists[r, 1].astype(jnp.int32)
-        columns = lists[r, 2].astype(jnp.int32)
-
-        def group_rows(k):
-            return tuple(
-                jnp.broadcast_to(table[i, k][None], (4, 8, LANES)).reshape(32, LANES)
-                for i in range(2)
-            )
-
-        slot_re, slot_im = lookup(group_rows, routes, 32)
-        slots[0] = slot_re
-        slots[1] = slot_im
-
-        def slot_rows(k):
-            return tuple(
-                jnp.broadcast_to(slots[i, k : k + 1, :], (32, LANES)) for i in range(2)
-            )
-
-        values = lookup(slot_rows, members, 32)
-        phase = columns & (RADIX - 1)
-        point = (columns >> 2).astype(F32)
+        members = lists[r, 1].astype(jnp.int32)[:size]
+        columns = lists[r, 2].astype(jnp.int32)[:size]
+        member_lane = members & (LANES - 1)
+        member_row = members >> 7
+        for s in range(4):
+            slots[2, 8 * s : 8 * s + 8, :] = routes[8 * s : 8 * s + 8].astype(F32)
+
+        def list_chunk(s, found):
+            route = slots[2, pl.ds(pl.multiple_of(8 * s, 8), 8), :].astype(jnp.int32)
+            route_lane = route & (LANES - 1)
+            route_row = route >> 7
+            slot = [jnp.zeros((8, LANES), F32) for _ in range(2)]
+            for k in range(32):
+                hit = route_row == k
+                slot = [
+                    jnp.where(hit, pick(table[i, k], route_lane), slot[i])
+                    for i in range(2)
+                ]
+            found = list(found)
+            for i in range(2):
+                slots[i, 0:8, :] = slot[i]
+            for k in range(8):
+                hit = member_row == 8 * s + k
+                for i in range(2):
+                    row = jnp.broadcast_to(slots[i, k : k + 1, :], (size, LANES))
+                    found[i] = jnp.where(hit, pick(row, member_lane), found[i])
+            return tuple(found)
+
+        nothing = jnp.zeros((size, LANES), F32)
+        values = lax.fori_loop(0, list_chunks, list_chunk, (nothing, nothing))
+        columns = columns & (NGRID - 1)
+        kind = (columns & (RADIX - 1)) + RADIX * (columns >> 9)
+        point = ((columns >> 2) & (LANES - 1)).astype(F32)
+        planes = [
+            jnp.where(kind == half * RADIX + qx, values[i], 0.0)
+            for half in range(2)
+            for qx in range(RADIX)
+            for i in range(2)
+        ]
+        cell = lax.broadcasted_iota(jnp.int32, (LANES, chunks * LANES), 0).astype(BF16)
         for qy in range(RADIX):
-            part = slice(8 * qy, 8 * qy + 8)
-            planes = [
-                jnp.where(phase[part] == qx, values[i][part], 0.0)
-                for qx in range(RADIX)
-                for i in range(2)
-            ]
             for h in range(2):
+                at = [8 * c + 2 * qy + h for c in range(chunks)]
                 left = jnp.concatenate(
                     [
                         jnp.concatenate(
                             [
                                 jnp.where(
-                                    own_row[s],
-                                    jnp.broadcast_to(
-                                        plane[4 * h + s : 4 * h + s + 1, :], (8, LANES)
-                                    ),
+                                    own_row,
+                                    jnp.broadcast_to(plane[a : a + 1, :], (8, LANES)),
                                     0.0,
                                 )
-                                for s in range(4)
+                                for a in at
                             ],
                             axis=1,
                         )
@@ -127,25 +127,30 @@
                     ],
                     axis=0,
                 ).astype(BF16)
-                spot = jnp.concatenate(
-                    [
-                        point[8 * qy + 4 * h + s : 8 * qy + 4 * h + s + 1, :]
-                        for s in range(4)
-                    ],
-                    axis=1,
-                ).astype(BF16)
-                onehot = jnp.where(cell == spot, BF16(1), BF16(0))
+                spot = jnp.concatenate([point[a : a + 1, :] for a in at], axis=1)
+                onehot = jnp.where(cell == spot.astype(BF16), BF16(1), BF16(0))
                 placed = lax.dot_general(
                     left, onehot, (((1,), (1,)), ((), ())), preferred_element_type=F32
                 )
                 start = pl.multiple_of(8 + r * slab_points + 8 * h, 8)
-                for qx in range(RADIX):
-                    for i in range(2):
-                        at = (qx * 2 + i) * 8
-                        for w in range(2):
-                            dense[i, qy, qx, w, pl.ds(start, 8), :] = placed[
-                                at : at + 8, w * LANES : (w + 1) * LANES
+                for half in range(2):
+                    for qx in range(RADIX):
+                        for i in range(2):
+                            a = ((half * RADIX + qx) * 2 + i) * 8
+                            dense[i, qy, qx, half, pl.ds(start, 8), :] = placed[
+                                a : a + 8, :
                             ]
+
+    def grid_slab(r, carry):
+        extent = lists[r, 2, 0:16, :].astype(jnp.int32)[0, 0] >> 10
+        row_chunks = extent & 3
+        list_chunks = (extent >> 2) + 1
+        for low, high in ((0, 1), (1, 2), (2, 4)):
+
+            @pl.when((row_chunks >= low) & (row_chunks < high))
+            def _():
+                grid_chunks(r, high, list_chunks)
+
         return carry
 
     lax.fori_loop(0, slabs, grid_slab, 0)
@@ -246,7 +251,7 @@
         out_specs=pl.BlockSpec(memory_space=pltpu.VMEM),
         scratch_shapes=[
             pltpu.VMEM((2, 32, 8, LANES), F32),
-            pltpu.VMEM((2, 32, LANES), F32),
+            pltpu.VMEM((3, 32, LANES), F32),
             pltpu.VMEM((2, RADIX, RADIX, 2, POINTS + 8, LANES), F32),
             pltpu.VMEM((NGRID, 2 * NGRID), BF16),
             pltpu.VMEM((NGRID, 2 * NGRID), BF16),
@@ -262,11 +267,14 @@
     slot = slot + (row_members & (LANES - 1))
     live = jnp.arange(row_members.shape[1], dtype=jnp.int32)[None, :] < row_counts[:, None]
     slot = jnp.where(live, slot, -1)
-    by_phase = [
-        a.reshape(-1, RADIX, a.shape[1]).transpose(1, 0, 2).reshape(32, LANES)
-        for a in (slot, anchor_cols)
+    row_chunks = jnp.clip((jnp.max(row_counts) + 15) // 16 - 1, 0, 3)
+    list_chunks = jnp.clip(jnp.max(slot) // 1024, 0, 3)
+    columns = anchor_cols + 1024 * (row_chunks + 4 * list_chunks)
+    ordered = [
+        a.reshape(2, 8, RADIX, 4, 16).transpose(3, 2, 0, 1, 4).reshape(32, LANES)
+        for a in (slot, columns)
     ]
-    return jnp.stack([routes.reshape(32, LANES), *by_phase]).astype(jnp.int16)
+    return jnp.stack([routes.reshape(32, LANES), *ordered]).astype(jnp.int16)
 
 
 def per_device(voltages, kernel, route_lists, row_members, row_counts, anchor_cols):

time: 111 us -> 106 us (0.955)
  Pallas kernels: 46.7 us -> 38.8 us
  between operations: 0.03 us -> 3.6 us
  waiting for transfers between devices: 3.55 us -> 0.01 us
  other arithmetic: 3.48 us -> 5.57 us
    pallas_call x1, Pallas kernels: 46.7 us -> 38.8 us  [sample_power(): pl.pallas_call(sample_kernel, out_shape=jax.ShapeDtypeStruct((NGRID, NGRI...]
    all_to_all x1, waiting for transfers between devices: 3.55 us -> 0.01 us  [per_device(): lax.all_to_all(mine, 'chan', split_axis=0, concat_axis=0, tiled=True)]
    reduce_max x0 -> x1, other arithmetic: none -> 1.37 us  [slab_lists(): row_chunks = jnp.clip((jnp.max(row_counts) + 15) // 16 - 1, 0, 3)]
  transfers between devices with their start and end apart: 1 -> 1, of which waited for: 1 -> 0; matrix products, arithmetic and copies ran while one was open for 2% -> 5% of each run, Pallas kernels for 0% -> 0%
where the time goes in v2:
time: 106 us
  blocking collectives  50.3 us (47%)
  Pallas kernels  38.8 us (37%)
  other arithmetic  5.57 us (5%)
  starting transfers between devices  4.38 us (4%)
  between operations  3.6 us (3%)
  local copies, waits for them, and re-layouts  2.99 us (3%)
    pallas_call x1, Pallas kernels, sample_power(): pl.pallas_call(sample_kernel, out_shape=jax.ShapeDtypeStruct((NGRID, NGRI...  38.8 us
    all_to_all x1, blocking collectives, per_device(): lax.all_to_all(power, 'row', split_axis=0, concat_axis=0, tiled=True)  31.6 us
    all_to_all x1, blocking collectives, per_device(): lax.all_to_all(lists, 'row', split_axis=0, concat_axis=0, tiled=True)  18.7 us
    all_to_all x1, starting transfers between devices, per_device(): lax.all_to_all(mine, 'chan', split_axis=0, concat_axis=0, tiled=True)  4.38 us
    another operation x3, other arithmetic  3.08 us
  transfers between devices with their start and end apart: 1, of which 0 were waited for; matrix products, arithmetic and copies ran while one was open for 5% of the time, Pallas kernels for 0%

profile of v2, /device:TPU:0, one launch (start us, length us, event | category | flops | bytes accessed | tf_op | source)
XLA Modules:
  0.0 105.7 jit_solution(13493261130231937552)
XLA Ops:
  0.0 0.0 copy-start
  0.0 1.6 %copy-done = bf16[8,16,2,4096]{3,2,1,0:T(2,128)(2,1)S(1)} copy-done((bf16[8,16,2,4096]{3,2,1,0:T(2,128)(2,1)S(1)}, bf16[8,16,2,4096]{3,2,1,0:T(2,128)(2,1)}, u32[]{:S(2)}) %copy-start) | copy-done | bytes 2097176
  1.6 0.1 constant_dynamic-slice_fusion
  1.7 0.8 reshape.44
  2.5 4.4 %all-to-all-start = ((bf16[8,2,32,128]{3,2,1,0:T(8,128)(2,1)}), bf16[8,2,32,128]{3,2,1,0:T(8,128)(2,1)S(1)}, u32[]{:S(2)}, u32[]{:S(2)}) async-start(bf16[8,2,32,128]{3,2,1,0:T(8,128)(2,1)} %reshape.44), calls=%async_computation | async-start | bytes 262144 | tf_op jit(solution)/shard_map/all_to_all | solution.py:290
  6.8 1.4 %reduce_max.18 = s32[]{:T(128)} reduce(s32[64]{0:T(128)} %param.12, s32[]{:T(128)} %constant.57.clone.1), dimensions={0}, to_apply=%region_0.1 | reduce | flops 63 | bytes 264 | tf_op jit(solution)/shard_map/reduce_max | solution.py:270
  8.9 1.6 %fusion.1 = (s16[64,64]{1,0:T(8,128)(2,1)S(1)}, s32[]{:T(128)}) fusion(s32[64,64]{1,0:T(8,128)} %param.11, s32[64]{0:T(128)} %param.12), kind=kLoop, calls=%fused_computation.9 | loop fusion | flops 49151 | bytes 24836 | tf_op jit(solution)/shard_map/convert.8
  13.3 0.8 add_convert_fusion
  14.0 0.8 convert_reduce_fusion.1
  14.8 0.1 reshape.46
  15.0 0.1 stack.11
  15.1 0.1 reshape.45
  15.2 0.1 stack.10
  15.3 0.0 all-to-all-done.volts
  15.4 0.0 copy-start.1
  15.4 0.1 broadcast_in_dim.16
  15.4 18.7 %all_to_all.15.lists = s16[16,3,32,128]{3,2,1,0:T(8,128)(2,1)} all-to-all(s16[16,3,32,128]{3,2,1,0:T(8,128)(2,1)S(1)} %broadcast_in_dim.16), channel_id=1, replica_groups=mesh['chan'=8,'row'=16] {'row'}, dimensions={0} | all-to-all | bytes 786432 | tf_op jit(solution)/shard_map/all_to_all | solution.py:287
  34.1 0.0 copy-done.1
  34.1 38.8 %shard_map.82 = bf16[1024,1024]{1,0:T(8,128)(2,1)} custom-call(f32[4,4]{1,0:T(4,128)} %bitcast.21, bf16[8,2,32,128]{3,2,1,0:T(8,128)(2,1)} %copy-done.1, s16[16,3,32,128]{3,2,1,0:T(8,128)(2,1)} %all_to_all.15.lists, bf16[4,512,512]{2,1,0:T(8,128)(2,1)} %constant.65.clone.wide, bf16[4,512,512]{2,1,0:T(8,128)(2,1)} %constant.66.clone.tall), custom_call_target="tpu_custom_call" | custom-call | tf_op jit(solution)/shard_map/pallas_call | solution.py:246
  72.9 31.6 %all_to_all.16 = bf16[16,64,1024]{2,1,0:T(8,128)(2,1)S(1)} all-to-all(bf16[16,64,1024]{2,1,0:T(8,128)(2,1)} %bitcast.16), channel_id=1, replica_groups=mesh['chan'=8,'row'=16] {'row'}, dimensions={0} | all-to-all | bytes 4194304 | tf_op jit(solution)/shard_map/all_to_all | solution.py:294
  104.5 0.4 convert_reduce_fusion
  104.9 0.7 multiply_bitcast_fusion
  (5 shorter events, 0.1 us)
Async XLA Ops:
  0.0 1.6 %copy-start = (bf16[8,16,2,4096]{3,2,1,0:T(2,128)(2,1)S(1)}, bf16[8,16,2,4096]{3,2,1,0:T(2,128)(2,1)}, u32[]{:S(2)}) copy-start(bf16[8,16,2,4096]{3,2,1,0:T(2,128)(2,1)} %param.8) | copy-start | bytes 6291460
  2.5 12.9 %all-to-all-start = ((bf16[8,2,32,128]{3,2,1,0:T(8,128)(2,1)}), bf16[8,2,32,128]{3,2,1,0:T(8,128)(2,1)S(1)}, u32[]{:S(2)}, u32[]{:S(2)}) async-start(bf16[8,2,32,128]{3,2,1,0:T(8,128)(2,1)} %reshape.44), calls=%async_computation | async-start | bytes 262144 | tf_op jit(solution)/shard_map/all_to_all | solution.py:290
  15.4 18.8 %copy-start.1 = (bf16[8,2,32,128]{3,2,1,0:T(8,128)(2,1)}, bf16[8,2,32,128]{3,2,1,0:T(8,128)(2,1)S(1)}, u32[]{:S(2)}) copy-start(bf16[8,2,32,128]{3,2,1,0:T(8,128)(2,1)S(1)} %all-to-all-done.volts) | copy-start | bytes 393220

commit v3 on v2

--- a/solution.py
+++ b/solution.py
@@ -45,15 +45,13 @@
 
 
 def sample_kernel(
-    taps, volts, lists, wide, tall, power, table, slots, dense, aperture, spectrum
+    taps, volts, lists, wide, tall, power, slots, dense, aperture, spectrum,
+    extent,
 ):
     slabs = lists.shape[0]
     groups = volts.shape[0]
     slab_points = POINTS // slabs
 
-    for g in range(groups):
-        for i in range(2):
-            table[i, :, g, :] = volts[g, i].astype(F32)
     for i in range(2):
         for qy in range(RADIX):
             for qx in range(RADIX):
@@ -64,40 +62,56 @@
     lane = lax.broadcasted_iota(jnp.int32, (8, LANES), 1)
     own_row = sub == lane >> 4
 
-    def grid_chunks(r, chunks, list_chunks):
+    for r in range(slabs):
+        extent[r] = lists[r, 2].astype(jnp.int32)[0, 0] >> 10
+
+    row_of = lax.broadcasted_iota(jnp.int32, (32, 2 * LANES), 0)
+    lane_of = lax.broadcasted_iota(jnp.int32, (LANES, 2 * LANES), 0).astype(BF16)
+
+    def gather_pair(pair, carry):
+        first, second = 2 * pair, 2 * pair + 1
+        routes = [lists[r, 0].astype(jnp.int32) for r in (first, second)]
+        last = jnp.maximum(extent[first] & 3, extent[second] & 3)
+        for s in range(4):
+
+            @pl.when(last >= s)
+            def _():
+                for g in range(groups):
+                    k = 8 * s + g
+                    route = jnp.concatenate([a[k : k + 1, :] for a in routes], axis=1)
+                    lane_spot = (route & (LANES - 1)).astype(F32).astype(BF16)
+                    onehot = jnp.where(lane_of == lane_spot, BF16(1), BF16(0))
+                    rows = jnp.dot(
+                        volts[g].reshape(64, LANES),
+                        onehot,
+                        preferred_element_type=F32,
+                    )
+                    hit = row_of == (route >> 7)
+                    for i in range(2):
+                        entry = jnp.sum(
+                            jnp.where(hit, rows[32 * i : 32 * i + 32], 0.0),
+                            axis=0,
+                            keepdims=True,
+                        )
+                        slots[i, first, k : k + 1, :] = entry[:, :LANES]
+                        slots[i, second, k : k + 1, :] = entry[:, LANES:]
+
+        return carry
+
+    lax.fori_loop(0, slabs // 2, gather_pair, 0)
+
+    def grid_chunks(r, chunks, list_rows):
         size = 8 * chunks
-        routes = lists[r, 0].astype(jnp.int32)
         members = lists[r, 1].astype(jnp.int32)[:size]
-        columns = lists[r, 2].astype(jnp.int32)[:size]
+        columns = lists[r, 2].astype(jnp.int32)[:size] & (NGRID - 1)
         member_lane = members & (LANES - 1)
         member_row = members >> 7
-        for s in range(4):
-            slots[2, 8 * s : 8 * s + 8, :] = routes[8 * s : 8 * s + 8].astype(F32)
-
-        def list_chunk(s, found):
-            route = slots[2, pl.ds(pl.multiple_of(8 * s, 8), 8), :].astype(jnp.int32)
-            route_lane = route & (LANES - 1)
-            route_row = route >> 7
-            slot = [jnp.zeros((8, LANES), F32) for _ in range(2)]
-            for k in range(32):
-                hit = route_row == k
-                slot = [
-                    jnp.where(hit, pick(table[i, k], route_lane), slot[i])
-                    for i in range(2)
-                ]
-            found = list(found)
+        values = [jnp.zeros((size, LANES), F32)] * 2
+        for k in range(list_rows):
+            hit = member_row == k
             for i in range(2):
-                slots[i, 0:8, :] = slot[i]
-            for k in range(8):
-                hit = member_row == 8 * s + k
-                for i in range(2):
-                    row = jnp.broadcast_to(slots[i, k : k + 1, :], (size, LANES))
-                    found[i] = jnp.where(hit, pick(row, member_lane), found[i])
-            return tuple(found)
-
-        nothing = jnp.zeros((size, LANES), F32)
-        values = lax.fori_loop(0, list_chunks, list_chunk, (nothing, nothing))
-        columns = columns & (NGRID - 1)
+                row = jnp.broadcast_to(slots[i, r, k : k + 1, :], (size, LANES))
+                values[i] = jnp.where(hit, pick(row, member_lane), values[i])
         kind = (columns & (RADIX - 1)) + RADIX * (columns >> 9)
         point = ((columns >> 2) & (LANES - 1)).astype(F32)
         planes = [
@@ -142,14 +156,13 @@
                             ]
 
     def grid_slab(r, carry):
-        extent = lists[r, 2, 0:16, :].astype(jnp.int32)[0, 0] >> 10
-        row_chunks = extent & 3
-        list_chunks = (extent >> 2) + 1
-        for low, high in ((0, 1), (1, 2), (2, 4)):
-
-            @pl.when((row_chunks >= low) & (row_chunks < high))
-            def _():
-                grid_chunks(r, high, list_chunks)
+        @pl.when(extent[r] < 4)
+        def _():
+            grid_chunks(r, 2, 16)
+
+        @pl.when(extent[r] >= 4)
+        def _():
+            grid_chunks(r, 4, 32)
 
         return carry
 
@@ -221,7 +234,7 @@
     lax.fori_loop(0, RADIX, row_transform, 0)
 
     def column_transform(n, carry):
-        rows = pl.ds(pl.multiple_of(n * 128, 128), 128)
+        rows = pl.ds(pl.multiple_of(n * 256, 256), 256)
         parts = [
             jnp.dot(
                 spectrum[rows, 2 * q * POINTS : 2 * (q + 1) * POINTS],
@@ -239,7 +252,7 @@
             ).astype(BF16)
         return carry
 
-    lax.fori_loop(0, NGRID // 128, column_transform, 0)
+    lax.fori_loop(0, NGRID // 256, column_transform, 0)
 
 
 def sample_power(taps, volts, lists, wide, tall, interpret=False):
@@ -250,13 +263,13 @@
         + [pl.BlockSpec(memory_space=pltpu.VMEM)] * 4,
         out_specs=pl.BlockSpec(memory_space=pltpu.VMEM),
         scratch_shapes=[
-            pltpu.VMEM((2, 32, 8, LANES), F32),
-            pltpu.VMEM((3, 32, LANES), F32),
+            pltpu.VMEM((2, lists.shape[0], 32, LANES), F32),
             pltpu.VMEM((2, RADIX, RADIX, 2, POINTS + 8, LANES), F32),
             pltpu.VMEM((NGRID, 2 * NGRID), BF16),
             pltpu.VMEM((NGRID, 2 * NGRID), BF16),
+            pltpu.SMEM((lists.shape[0],), jnp.int32),
         ],
-        compiler_params=pltpu.CompilerParams(vmem_limit_bytes=56 * 2**20),
+        compiler_params=pltpu.CompilerParams(vmem_limit_bytes=40 * 2**20),
         interpret=interpret,
     )(taps, volts, lists, wide, tall)
 
@@ -267,9 +280,10 @@
     slot = slot + (row_members & (LANES - 1))
     live = jnp.arange(row_members.shape[1], dtype=jnp.int32)[None, :] < row_counts[:, None]
     slot = jnp.where(live, slot, -1)
-    row_chunks = jnp.clip((jnp.max(row_counts) + 15) // 16 - 1, 0, 3)
-    list_chunks = jnp.clip(jnp.max(slot) // 1024, 0, 3)
-    columns = anchor_cols + 1024 * (row_chunks + 4 * list_chunks)
+    top = jnp.max(slot)
+    wide = (jnp.max(row_counts) > 32) | (top >= 2048)
+    extent = (jnp.maximum(top, 0) >> 10) + jnp.where(wide, 4, 0)
+    columns = anchor_cols + 1024 * extent
     ordered = [
         a.reshape(2, 8, RADIX, 4, 16).transpose(3, 2, 0, 1, 4).reshape(32, LANES)
         for a in (slot, columns)

time: 106 us -> 99.9 us (0.942)
  Pallas kernels: 38.8 us -> 31.8 us
  local copies, waits for them, and re-layouts: 2.99 us -> 6.17 us
  between operations: 3.6 us -> 1.91 us
    pallas_call x1, Pallas kernels: 38.8 us -> 31.8 us  [sample_power(): pl.pallas_call(sample_kernel, out_shape=jax.ShapeDtypeStruct((NGRID, NGRI...]
    unnamed x4 -> x8, local copies, waits for them, and re-layouts: 1.6 us -> 4.77 us
where the time goes in v3:
time: 99.9 us; the launch traced here: 99.3 us
  blocking collectives  49.6 us (50%)
  Pallas kernels  31.8 us (32%)
  local copies, waits for them, and re-layouts  6.17 us (6%)
  other arithmetic  5.48 us (5%)
  starting transfers between devices  4.38 us (4%)
  between operations  1.91 us (2%)
    pallas_call x1, Pallas kernels, sample_power(): pl.pallas_call(sample_kernel, out_shape=jax.ShapeDtypeStruct((NGRID, NGRI...  31.8 us
    all_to_all x1, blocking collectives, per_device(): lax.all_to_all(power, 'row', split_axis=0, concat_axis=0, tiled=True)  31 us
    all_to_all x1, blocking collectives, per_device(): lax.all_to_all(lists, 'row', split_axis=0, concat_axis=0, tiled=True)  18.6 us
    unnamed x8, local copies, waits for them, and re-layouts  4.77 us
    all_to_all x1, starting transfers between devices, per_device(): lax.all_to_all(mine, 'chan', split_axis=0, concat_axis=0, tiled=True)  4.38 us
    another operation x3, other arithmetic  2.99 us
  transfers between devices with their start and end apart: 1, of which 0 were waited for; matrix products, arithmetic and copies ran while one was open for 5% of the time, Pallas kernels for 0%

profile of v3, /device:TPU:0, one launch (start us, length us, event | category | flops | bytes accessed | tf_op | source)
XLA Modules:
  0.0 99.3 jit_solution(5444014548793388495)
XLA Ops:
  0.0 0.0 copy-start
  0.0 0.0 copy-start.3
  0.0 1.6 %copy-done = bf16[8,16,2,4096]{3,2,1,0:T(2,128)(2,1)S(1)} copy-done((bf16[8,16,2,4096]{3,2,1,0:T(2,128)(2,1)S(1)}, bf16[8,16,2,4096]{3,2,1,0:T(2,128)(2,1)}, u32[]{:S(2)}) %copy-start) | copy-done | bytes 2097176
  1.6 0.1 constant_dynamic-slice_fusion
  1.7 0.8 reshape.44
  2.5 4.4 %all-to-all-start = ((bf16[8,2,32,128]{3,2,1,0:T(8,128)(2,1)}), bf16[8,2,32,128]{3,2,1,0:T(8,128)(2,1)S(1)}, u32[]{:S(2)}, u32[]{:S(2)}) async-start(bf16[8,2,32,128]{3,2,1,0:T(8,128)(2,1)} %reshape.44), calls=%async_computation | async-start | bytes 262144 | tf_op jit(solution)/shard_map/all_to_all | solution.py:304
  6.8 1.4 %reduce_max.19 = s32[]{:T(128)} reduce(s32[64]{0:T(128)} %param.12, s32[]{:T(128)} %constant.12.clone.1), dimensions={0}, to_apply=%region_1.2 | reduce | flops 63 | bytes 264 | tf_op jit(solution)/shard_map/reduce_max | solution.py:284
  8.2 1.5 %fusion.1 = (s16[64,64]{1,0:T(8,128)(2,1)S(1)}, s32[]{:T(128)}) fusion(s32[64,64]{1,0:T(8,128)} %param.11, s32[64]{0:T(128)} %param.12), kind=kLoop, calls=%fused_computation.9 | loop fusion | flops 49151 | bytes 24836 | tf_op jit(solution)/shard_map/convert.8
  11.5 0.8 add_convert_fusion
  12.3 0.8 convert_reduce_fusion.1
  13.0 0.1 reshape.46
  13.2 0.1 stack.11
  13.3 0.1 reshape.45
  13.4 0.1 stack.10
  13.6 0.0 all-to-all-done.volts
  13.6 0.1 broadcast_in_dim.16
  13.6 18.6 %all_to_all.15.lists = s16[16,3,32,128]{3,2,1,0:T(8,128)(2,1)S(1)} all-to-all(s16[16,3,32,128]{3,2,1,0:T(8,128)(2,1)S(1)} %broadcast_in_dim.16), channel_id=1, replica_groups=mesh['chan'=8,'row'=16] {'row'}, dimensions={0} | all-to-all | bytes 786432 | tf_op jit(solution)/shard_map/all_to_all | solution.py:301
  32.2 0.0 copy-done.3
  32.2 0.0 copy-start.1
  32.2 1.6 %copy-done.1 = bf16[4,512,512]{2,1,0:T(8,128)(2,1)S(1)} copy-done((bf16[4,512,512]{2,1,0:T(8,128)(2,1)S(1)}, bf16[4,512,512]{2,1,0:T(8,128)(2,1)}, u32[]{:S(2)}) %copy-start.1) | copy-done | bytes 2097176
  33.8 0.0 copy-start.2
  33.8 1.6 %copy-done.2 = bf16[4,512,512]{2,1,0:T(8,128)(2,1)S(1)} copy-done((bf16[4,512,512]{2,1,0:T(8,128)(2,1)S(1)}, bf16[4,512,512]{2,1,0:T(8,128)(2,1)}, u32[]{:S(2)}) %copy-start.2) | copy-done | bytes 2097176
  35.4 31.8 %shard_map.82 = bf16[1024,1024]{1,0:T(8,128)(2,1)S(1)} custom-call(f32[4,4]{1,0:T(4,128)S(1)} %bitcast.17, bf16[8,2,32,128]{3,2,1,0:T(8,128)(2,1)S(1)} %all-to-all-done.volts, s16[16,3,32,128]{3,2,1,0:T(8,128)(2,1)S(1)} %all_to_all.15.lists, bf16[4,512,512]{2,1,0:T(8,128)(2,1)S(1)} %copy-done.2, bf16[4,512,512]{2,1,0:T(8,128)(2,1)S(1)} %copy-done.1), custom_call_target="tpu_custom_call" | custom-call | tf_op jit(solution)/shard_map/pallas_call | solution.py:259
  67.2 31.0 %all_to_all.16 = bf16[16,64,1024]{2,1,0:T(8,128)(2,1)S(1)} all-to-all(bf16[16,64,1024]{2,1,0:T(8,128)(2,1)S(1)} %bitcast.16), channel_id=1, replica_groups=mesh['chan'=8,'row'=16] {'row'}, dimensions={0} | all-to-all | bytes 4194304 | tf_op jit(solution)/shard_map/all_to_all | solution.py:308
  98.2 0.4 convert_reduce_fusion
  98.6 0.7 multiply_bitcast_fusion
  (5 shorter events, 0.1 us)
Async XLA Ops:
  0.0 1.6 %copy-start = (bf16[8,16,2,4096]{3,2,1,0:T(2,128)(2,1)S(1)}, bf16[8,16,2,4096]{3,2,1,0:T(2,128)(2,1)}, u32[]{:S(2)}) copy-start(bf16[8,16,2,4096]{3,2,1,0:T(2,128)(2,1)} %param.8) | copy-start | bytes 6291460
  0.0 32.2 %copy-start.3 = (f32[1,4,4]{2,1,0:T(4,128)S(1)}, f32[1,4,4]{2,1,0:T(4,128)}, u32[]{:S(2)}) copy-start(f32[1,4,4]{2,1,0:T(4,128)} %param.9) | copy-start | bytes 196
  2.5 11.1 %all-to-all-start = ((bf16[8,2,32,128]{3,2,1,0:T(8,128)(2,1)}), bf16[8,2,32,128]{3,2,1,0:T(8,128)(2,1)S(1)}, u32[]{:S(2)}, u32[]{:S(2)}) async-start(bf16[8,2,32,128]{3,2,1,0:T(8,128)(2,1)} %reshape.44), calls=%async_computation | async-start | bytes 262144 | tf_op jit(solution)/shard_map/all_to_all | solution.py:304
  32.2 1.6 %copy-start.1 = (bf16[4,512,512]{2,1,0:T(8,128)(2,1)S(1)}, bf16[4,512,512]{2,1,0:T(8,128)(2,1)}, u32[]{:S(2)}) copy-start(bf16[4,512,512]{2,1,0:T(8,128)(2,1)} %constant.45.clone.tall) | copy-start | bytes 6291460
  33.8 1.6 %copy-start.2 = (bf16[4,512,512]{2,1,0:T(8,128)(2,1)S(1)}, bf16[4,512,512]{2,1,0:T(8,128)(2,1)}, u32[]{:S(2)}) copy-start(bf16[4,512,512]{2,1,0:T(8,128)(2,1)} %constant.44.clone.wide) | copy-start | bytes 6291460

commit v4 on v3

--- a/solution.py
+++ b/solution.py
@@ -45,12 +45,16 @@
 
 
 def sample_kernel(
-    taps, volts, lists, wide, tall, power, slots, dense, aperture, spectrum,
-    extent,
+    taps, extent, volts, lists, wide_from, tall_from, power, slots, dense, aperture,
+    spectrum, wide, tall, arrived,
 ):
     slabs = lists.shape[0]
     groups = volts.shape[0]
     slab_points = POINTS // slabs
+    wide_copy = pltpu.make_async_copy(wide_from, wide, arrived.at[0])
+    tall_copy = pltpu.make_async_copy(tall_from, tall, arrived.at[1])
+    wide_copy.start()
+    tall_copy.start()
 
     for i in range(2):
         for qy in range(RADIX):
@@ -61,9 +65,6 @@
     sub = lax.broadcasted_iota(jnp.int32, (8, LANES), 0)
     lane = lax.broadcasted_iota(jnp.int32, (8, LANES), 1)
     own_row = sub == lane >> 4
-
-    for r in range(slabs):
-        extent[r] = lists[r, 2].astype(jnp.int32)[0, 0] >> 10
 
     row_of = lax.broadcasted_iota(jnp.int32, (32, 2 * LANES), 0)
     lane_of = lax.broadcasted_iota(jnp.int32, (LANES, 2 * LANES), 0).astype(BF16)
@@ -103,7 +104,7 @@
     def grid_chunks(r, chunks, list_rows):
         size = 8 * chunks
         members = lists[r, 1].astype(jnp.int32)[:size]
-        columns = lists[r, 2].astype(jnp.int32)[:size] & (NGRID - 1)
+        columns = lists[r, 2].astype(jnp.int32)[:size]
         member_lane = members & (LANES - 1)
         member_row = members >> 7
         values = [jnp.zeros((size, LANES), F32)] * 2
@@ -231,6 +232,7 @@
             ] = im[m].astype(BF16)
         return carry
 
+    wide_copy.wait()
     lax.fori_loop(0, RADIX, row_transform, 0)
 
     def column_transform(n, carry):
@@ -252,26 +254,29 @@
             ).astype(BF16)
         return carry
 
+    tall_copy.wait()
     lax.fori_loop(0, NGRID // 256, column_transform, 0)
 
 
-def sample_power(taps, volts, lists, wide, tall, interpret=False):
+def sample_power(taps, extent, volts, lists, wide, tall):
     return pl.pallas_call(
         sample_kernel,
         out_shape=jax.ShapeDtypeStruct((NGRID, NGRID), BF16),
-        in_specs=[pl.BlockSpec(memory_space=pltpu.SMEM)]
-        + [pl.BlockSpec(memory_space=pltpu.VMEM)] * 4,
+        in_specs=[pl.BlockSpec(memory_space=pltpu.SMEM)] * 2
+        + [pl.BlockSpec(memory_space=pltpu.VMEM)] * 2
+        + [pl.BlockSpec(memory_space=pl.ANY)] * 2,
         out_specs=pl.BlockSpec(memory_space=pltpu.VMEM),
         scratch_shapes=[
             pltpu.VMEM((2, lists.shape[0], 32, LANES), F32),
             pltpu.VMEM((2, RADIX, RADIX, 2, POINTS + 8, LANES), F32),
             pltpu.VMEM((NGRID, 2 * NGRID), BF16),
             pltpu.VMEM((NGRID, 2 * NGRID), BF16),
-            pltpu.SMEM((lists.shape[0],), jnp.int32),
+            pltpu.VMEM(wide.shape, BF16),
+            pltpu.VMEM(tall.shape, BF16),
+            pltpu.SemaphoreType.DMA((2,)),
         ],
-        compiler_params=pltpu.CompilerParams(vmem_limit_bytes=40 * 2**20),
-        interpret=interpret,
-    )(taps, volts, lists, wide, tall)
+        compiler_params=pltpu.CompilerParams(vmem_limit_bytes=56 * 2**20),
+    )(taps, extent, volts, lists, wide, tall)
 
 
 def slab_lists(route_lists, row_members, row_counts, anchor_cols):
@@ -280,15 +285,19 @@
     slot = slot + (row_members & (LANES - 1))
     live = jnp.arange(row_members.shape[1], dtype=jnp.int32)[None, :] < row_counts[:, None]
     slot = jnp.where(live, slot, -1)
-    top = jnp.max(slot)
-    wide = (jnp.max(row_counts) > 32) | (top >= 2048)
-    extent = (jnp.maximum(top, 0) >> 10) + jnp.where(wide, 4, 0)
-    columns = anchor_cols + 1024 * extent
     ordered = [
         a.reshape(2, 8, RADIX, 4, 16).transpose(3, 2, 0, 1, 4).reshape(32, LANES)
-        for a in (slot, columns)
+        for a in (slot, anchor_cols)
     ]
     return jnp.stack([routes.reshape(32, LANES), *ordered]).astype(jnp.int16)
+
+
+def list_extents(lists):
+    slot = lists[:, 1].astype(jnp.int32)
+    top = jnp.max(slot, axis=(1, 2))
+    late = jnp.max(slot[:, 16:], axis=(1, 2))
+    wide = (top >= 2048) | (late >= 0)
+    return (jnp.maximum(top, 0) >> 10) + jnp.where(wide, 4, 0)
 
 
 def per_device(voltages, kernel, route_lists, row_members, row_counts, anchor_cols):
@@ -301,9 +310,17 @@
     lists = lax.all_to_all(lists, "row", split_axis=0, concat_axis=0, tiled=True)
     mine = lax.dynamic_index_in_dim(voltages, lax.axis_index("row"), 1, keepdims=False)
     mine = mine.reshape(chan_count, 2, group_size // LANES, LANES)
+    lists, mine = lax.optimization_barrier((lists, mine))
     volts = lax.all_to_all(mine, "chan", split_axis=0, concat_axis=0, tiled=True)
     wide, tall = stage_tables()
-    power = sample_power(kernel[0], volts, lists, jnp.asarray(wide), jnp.asarray(tall))
+    power = sample_power(
+        kernel[0],
+        list_extents(lists),
+        volts,
+        lists,
+        jnp.asarray(wide),
+        jnp.asarray(tall),
+    )
     power = power.reshape(row_count, NGRID // row_count, NGRID)
     power = lax.all_to_all(power, "row", split_axis=0, concat_axis=0, tiled=True)
     scale_factor = 1.0 / (group_size * chan_count * samples * KERNEL_SIDE * KERNEL_SIDE)

time: 99.9 us -> 101 us (1.011)
  blocking collectives: 49.6 us -> 32.1 us
  waiting for transfers between devices: 0.01 us -> 14.4 us
  starting transfers between devices: 4.38 us -> 12.4 us
  local copies, waits for them, and re-layouts: 6.17 us -> 2.79 us
  Pallas kernels: 31.8 us -> 33.6 us
  between operations: 1.91 us -> 0.11 us
    all_to_all x1 -> x0, blocking collectives: 18.6 us -> none  [per_device(): lax.all_to_all(lists, 'row', split_axis=0, concat_axis=0, tiled=True)]
    all_to_all x0 -> x1, waiting for transfers between devices: none -> 9.2 us  [per_device(): lax.all_to_all(lists, 'row', split_axis=0, concat_axis=0, tiled=True)]
    all_to_all x0 -> x1, starting transfers between devices: none -> 8.13 us  [per_device(): lax.all_to_all(lists, 'row', split_axis=0, concat_axis=0, tiled=True)]
    all_to_all x1, waiting for transfers between devices: 0.01 us -> 5.18 us  [per_device(): lax.all_to_all(mine, 'chan', split_axis=0, concat_axis=0, tiled=True)]
    unnamed x8 -> x6, local copies, waits for them, and re-layouts: 4.77 us -> 0.66 us
    pallas_call x1, Pallas kernels: 31.8 us -> 33.6 us  [sample_power(): pl.pallas_call(sample_kernel, out_shape=jax.ShapeDtypeStruct((NGRID, NGRI...]
    all_to_all x1, blocking collectives: 31 us -> 32.1 us  [per_device(): lax.all_to_all(power, 'row', split_axis=0, concat_axis=0, tiled=True)]
  transfers between devices with their start and end apart: 1 -> 2, of which waited for: 0 -> 2; matrix products, arithmetic and copies ran while one was open for 5% -> 2% of each run, Pallas kernels for 0% -> 0%
where the time goes in v4:
time: 101 us; the launch traced here: 100 us
  Pallas kernels  33.6 us (33%)
  blocking collectives  32.1 us (32%)
  waiting for transfers between devices  14.4 us (14%)
  starting transfers between devices  12.4 us (12%)
  other arithmetic  5.01 us (5%)
  local copies, waits for them, and re-layouts  2.79 us (3%)
    pallas_call x1, Pallas kernels, sample_power(): pl.pallas_call(sample_kernel, out_shape=jax.ShapeDtypeStruct((NGRID, NGRI...  33.6 us
    all_to_all x1, blocking collectives, per_device(): lax.all_to_all(power, 'row', split_axis=0, concat_axis=0, tiled=True)  32.1 us
    all_to_all x1, waiting for transfers between devices, per_device(): lax.all_to_all(lists, 'row', split_axis=0, concat_axis=0, tiled=True)  9.2 us
    all_to_all x1, starting transfers between devices, per_device(): lax.all_to_all(lists, 'row', split_axis=0, concat_axis=0, tiled=True)  8.13 us
    all_to_all x1, waiting for transfers between devices, per_device(): lax.all_to_all(mine, 'chan', split_axis=0, concat_axis=0, tiled=True)  5.18 us
    all_to_all x1, starting transfers between devices, per_device(): lax.all_to_all(mine, 'chan', split_axis=0, concat_axis=0, tiled=True)  4.31 us
    another operation x3, other arithmetic  2.51 us
  transfers between devices with their start and end apart: 2, of which 2 were waited for; matrix products, arithmetic and copies ran while one was open for 2% of the time, Pallas kernels for 0%

profile of v4, /device:TPU:0, one launch (start us, length us, event | category | flops | bytes accessed | tf_op | source)
XLA Modules:
  0.0 100.4 jit_solution(18233662112054913781)
XLA Ops:
  0.0 0.0 copy-start
  0.0 0.9 convert_reduce_fusion.2
  0.9 0.8 convert.20
  1.7 0.1 reshape.46
  1.8 0.1 stack.11
  2.0 0.8 select_convert_fusion
  2.8 0.1 reshape.45
  2.9 0.1 stack.10
  3.1 0.8 broadcast_in_dim.22
  3.8 8.1 %all-to-all-start = ((s16[16,3,32,128]{3,2,1,0:T(8,128)(2,1)}), s16[16,3,32,128]{3,2,1,0:T(8,128)(2,1)S(1)}, u32[]{:S(2)}, u32[]{:S(2)}) async-start(s16[16,3,32,128]{3,2,1,0:T(8,128)(2,1)} %broadcast_in_dim.22), calls=%async_computation | async-start | bytes 786432 | tf_op jit(solution)/shard_map/all_to_all | solution.py:310
  12.0 0.0 copy-done
  12.0 0.1 constant_dynamic-slice_fusion
  12.1 0.8 reshape.47
  12.9 9.2 %all-to-all-done.lists = s16[16,3,32,128]{3,2,1,0:T(8,128)(2,1)S(1)} async-done(((s16[16,3,32,128]{3,2,1,0:T(8,128)(2,1)}), s16[16,3,32,128]{3,2,1,0:T(8,128)(2,1)S(1)}, u32[]{:S(2)}, u32[]{:S(2)}) %all-to-all-start) | async-done | bytes 393248 | tf_op jit(solution)/shard_map/all_to_all | solution.py:310
  22.1 0.0 copy-start.1
  22.1 0.4 convert_reduce_fusion.1
  22.5 4.3 %all-to-all-start.1 = ((bf16[8,2,32,128]{3,2,1,0:T(8,128)(2,1)}), bf16[8,2,32,128]{3,2,1,0:T(8,128)(2,1)S(1)}, u32[]{:S(2)}, u32[]{:S(2)}) async-start(bf16[8,2,32,128]{3,2,1,0:T(8,128)(2,1)} %reshape.47), calls=%async_computation.1 | async-start | bytes 262144 | tf_op jit(solution)/shard_map/all_to_all | solution.py:314
  26.8 0.4 slice_reduce_fusion
  27.2 0.6 fusion.extent
  27.8 5.2 %all-to-all-done.1.volts = bf16[8,2,32,128]{3,2,1,0:T(8,128)(2,1)S(1)} async-done(((bf16[8,2,32,128]{3,2,1,0:T(8,128)(2,1)}), bf16[8,2,32,128]{3,2,1,0:T(8,128)(2,1)S(1)}, u32[]{:S(2)}, u32[]{:S(2)}) %all-to-all-start.1) | async-done | bytes 131104 | tf_op jit(solution)/shard_map/all_to_all | solution.py:314
  33.0 0.0 copy-start.2
  33.0 0.0 copy-done.1
  33.0 0.7 copy-done.2
  33.6 33.6 %shard_map.82 = bf16[1024,1024]{1,0:T(8,128)(2,1)} custom-call(f32[4,4]{1,0:T(4,128)} %bitcast.23, s32[16]{0:T(128)} %fusion.extent, bf16[8,2,32,128]{3,2,1,0:T(8,128)(2,1)} %copy-done.2, s16[16,3,32,128]{3,2,1,0:T(8,128)(2,1)} %copy-done.1, bf16[4,512,512]{2,1,0:T(8,128)(2,1)} %constant.42.clone.wide_from, bf16[4,512,512]{2,1,0:T(8,128)(2,1)} %constant.43.clone.tall_from), custom_call_target="tpu_custom_call" | custom-call | tf_op jit(solution)/shard_map/pallas_call | solution.py:262
  67.2 32.1 %all_to_all.15 = bf16[16,64,1024]{2,1,0:T(8,128)(2,1)S(1)} all-to-all(bf16[16,64,1024]{2,1,0:T(8,128)(2,1)} %bitcast.18), channel_id=1, replica_groups=mesh['chan'=8,'row'=16] {'row'}, dimensions={0} | all-to-all | bytes 4194304 | tf_op jit(solution)/shard_map/all_to_all | solution.py:325
  99.3 0.4 convert_reduce_fusion
  99.7 0.7 multiply_bitcast_fusion
  (6 shorter events, 0.1 us)
Async XLA Ops:
  0.0 12.0 %copy-start = (bf16[8,16,2,4096]{3,2,1,0:T(2,128)(2,1)S(1)}, bf16[8,16,2,4096]{3,2,1,0:T(2,128)(2,1)}, u32[]{:S(2)}) copy-start(bf16[8,16,2,4096]{3,2,1,0:T(2,128)(2,1)} %param.8) | copy-start | bytes 6291460
  3.8 18.2 %all-to-all-start = ((s16[16,3,32,128]{3,2,1,0:T(8,128)(2,1)}), s16[16,3,32,128]{3,2,1,0:T(8,128)(2,1)S(1)}, u32[]{:S(2)}, u32[]{:S(2)}) async-start(s16[16,3,32,128]{3,2,1,0:T(8,128)(2,1)} %broadcast_in_dim.22), calls=%async_computation | async-start | bytes 786432 | tf_op jit(solution)/shard_map/all_to_all | solution.py:310
  22.1 10.9 %copy-start.1 = (s16[16,3,32,128]{3,2,1,0:T(8,128)(2,1)}, s16[16,3,32,128]{3,2,1,0:T(8,128)(2,1)S(1)}, u32[]{:S(2)}) copy-start(s16[16,3,32,128]{3,2,1,0:T(8,128)(2,1)S(1)} %all-to-all-done.lists) | copy-start | bytes 1179652
  22.5 10.4 %all-to-all-start.1 = ((bf16[8,2,32,128]{3,2,1,0:T(8,128)(2,1)}), bf16[8,2,32,128]{3,2,1,0:T(8,128)(2,1)S(1)}, u32[]{:S(2)}, u32[]{:S(2)}) async-start(bf16[8,2,32,128]{3,2,1,0:T(8,128)(2,1)} %reshape.47), calls=%async_computation.1 | async-start | bytes 262144 | tf_op jit(solution)/shard_map/all_to_all | solution.py:314
  33.0 0.7 copy-start.2

commit v5 on v4

--- a/solution.py
+++ b/solution.py
@@ -8,6 +8,7 @@
 
 NGRID = 1024
 KERNEL_SIDE = 4
+SLAB = 64
 RADIX = 4
 POINTS = NGRID // RADIX
 LANES = 128
@@ -45,7 +46,7 @@
 
 
 def sample_kernel(
-    taps, extent, volts, lists, wide_from, tall_from, power, slots, dense, aperture,
+    taps, extent, volts, lists, wide_from, tall_from, power, slots, bands, cells, aperture,
     spectrum, wide, tall, arrived,
 ):
     slabs = lists.shape[0]
@@ -56,15 +57,25 @@
     wide_copy.start()
     tall_copy.start()
 
-    for i in range(2):
-        for qy in range(RADIX):
-            for qx in range(RADIX):
-                for w in range(2):
-                    dense[i, qy, qx, w, 0:8, :] = jnp.zeros((8, LANES), F32)
+    down = lax.broadcasted_iota(jnp.int32, (SLAB, 4 * SLAB), 0)
+    across = lax.broadcasted_iota(jnp.int32, (SLAB, 4 * SLAB), 1)
+    apart = RADIX * (down & 15) + (down >> 4)
+    apart = apart - RADIX * (across & 15) - ((across >> 4) & 3)
+    apart = apart + SLAB * ((across >> 6) & 1)
+    for kx in range(KERNEL_SIDE):
+        tap = jnp.zeros((SLAB, 4 * SLAB), F32)
+        for ky in range(KERNEL_SIDE):
+            tap = jnp.where(apart == ky, taps[ky, kx], tap)
+        high = tap.astype(BF16).astype(F32)
+        bands[kx * SLAB : (kx + 1) * SLAB, :] = jnp.where(
+            across < 2 * SLAB, high, tap - high
+        ).astype(BF16)
+    cells[2] = jnp.zeros(cells.shape[1:], BF16)
 
     sub = lax.broadcasted_iota(jnp.int32, (8, LANES), 0)
     lane = lax.broadcasted_iota(jnp.int32, (8, LANES), 1)
     own_row = sub == lane >> 4
+    first_lane = lax.broadcasted_iota(jnp.int32, (SLAB, POINTS), 1) == 0
 
     row_of = lax.broadcasted_iota(jnp.int32, (32, 2 * LANES), 0)
     lane_of = lax.broadcasted_iota(jnp.int32, (LANES, 2 * LANES), 0).astype(BF16)
@@ -101,7 +112,41 @@
 
     lax.fori_loop(0, slabs // 2, gather_pair, 0)
 
+    def convolve(r):
+        here = lax.rem(r + 3, 3)
+        before = lax.rem(r + 2, 3)
+        for i in range(2):
+            sums = []
+            for q in range(RADIX):
+                rows = [cells[here, 2 * q + i], cells[before, 2 * q + i]]
+                sums.append(
+                    jnp.dot(
+                        bands[...],
+                        jnp.concatenate(rows + rows, axis=0),
+                        preferred_element_type=F32,
+                    )
+                )
+            for qx in range(RADIX):
+                terms = [
+                    sums[(qx - kx) % RADIX][kx * SLAB : (kx + 1) * SLAB]
+                    for kx in range(KERNEL_SIDE)
+                ]
+                total = sum(terms[1 : qx + 1], terms[0])
+                if qx < KERNEL_SIDE - 1:
+                    spill = sum(terms[qx + 2 :], terms[qx + 1])
+                    spill = pltpu.roll(spill, 1, 1)
+                    total = total + jnp.where(first_lane, 0.0, spill)
+                total = total.astype(BF16)
+                at = (2 * qx + i) * POINTS
+                for qy in range(RADIX):
+                    row = pl.multiple_of(qy * POINTS + slab_points * jnp.maximum(r, 0), 16)
+                    aperture[pl.ds(row, 16), at : at + POINTS] = total[
+                        16 * qy : 16 * qy + 16
+                    ]
+
     def grid_chunks(r, chunks, list_rows):
+        convolve(r - 1)
+        place = lax.rem(r, 3)
         size = 8 * chunks
         members = lists[r, 1].astype(jnp.int32)[:size]
         columns = lists[r, 2].astype(jnp.int32)[:size]
@@ -123,6 +168,7 @@
         ]
         cell = lax.broadcasted_iota(jnp.int32, (LANES, chunks * LANES), 0).astype(BF16)
         for qy in range(RADIX):
+            placed = []
             for h in range(2):
                 at = [8 * c + 2 * qy + h for c in range(chunks)]
                 left = jnp.concatenate(
@@ -144,17 +190,25 @@
                 ).astype(BF16)
                 spot = jnp.concatenate([point[a : a + 1, :] for a in at], axis=1)
                 onehot = jnp.where(cell == spot.astype(BF16), BF16(1), BF16(0))
-                placed = lax.dot_general(
-                    left, onehot, (((1,), (1,)), ((), ())), preferred_element_type=F32
+                placed.append(
+                    lax.dot_general(
+                        left,
+                        onehot,
+                        (((1,), (1,)), ((), ())),
+                        preferred_element_type=F32,
+                    )
                 )
-                start = pl.multiple_of(8 + r * slab_points + 8 * h, 8)
-                for half in range(2):
-                    for qx in range(RADIX):
-                        for i in range(2):
-                            a = ((half * RADIX + qx) * 2 + i) * 8
-                            dense[i, qy, qx, half, pl.ds(start, 8), :] = placed[
-                                a : a + 8, :
-                            ]
+            for half in range(2):
+                for plane in range(2 * RADIX):
+                    a = (half * 2 * RADIX + plane) * 8
+                    cells[
+                        place,
+                        plane,
+                        16 * qy : 16 * qy + 16,
+                        half * LANES : (half + 1) * LANES,
+                    ] = jnp.concatenate([p[a : a + 8, :] for p in placed], axis=0).astype(
+                        BF16
+                    )
 
     def grid_slab(r, carry):
         @pl.when(extent[r] < 4)
@@ -168,45 +222,7 @@
         return carry
 
     lax.fori_loop(0, slabs, grid_slab, 0)
-
-    first_lane = lax.broadcasted_iota(jnp.int32, (16, POINTS), 1) == 0
-
-    def convolve(t, carry):
-        for i in range(2):
-            for qy in range(RADIX):
-                sums = [jnp.zeros((16, POINTS), F32) for _ in range(RADIX)]
-                for ky in range(KERNEL_SIDE):
-                    source = (qy - ky) % RADIX
-                    start = 8 + 16 * t - (1 if ky > qy else 0)
-                    here = [
-                        jnp.concatenate(
-                            [
-                                dense[i, source, qx, w, pl.ds(start, 16), :]
-                                for w in range(2)
-                            ],
-                            axis=1,
-                        )
-                        for qx in range(RADIX)
-                    ]
-                    before = [
-                        None
-                        if qx == 0
-                        else jnp.where(first_lane, 0.0, pltpu.roll(here[qx], 1, 1))
-                        for qx in range(RADIX)
-                    ]
-                    for qx in range(RADIX):
-                        for kx in range(KERNEL_SIDE):
-                            near = before if kx > qx else here
-                            sums[qx] = (
-                                sums[qx] + taps[ky, kx] * near[(qx - kx) % RADIX]
-                            )
-                row = pl.multiple_of(qy * POINTS + 16 * t, 16)
-                for qx in range(RADIX):
-                    at = (2 * qx + i) * POINTS
-                    aperture[pl.ds(row, 16), at : at + POINTS] = sums[qx].astype(BF16)
-        return carry
-
-    lax.fori_loop(0, POINTS // 16, convolve, 0)
+    convolve(slabs - 1)
 
     def row_transform(qy, carry):
         rows = pl.ds(pl.multiple_of(qy * POINTS, POINTS), POINTS)
@@ -268,7 +284,8 @@
         out_specs=pl.BlockSpec(memory_space=pltpu.VMEM),
         scratch_shapes=[
             pltpu.VMEM((2, lists.shape[0], 32, LANES), F32),
-            pltpu.VMEM((2, RADIX, RADIX, 2, POINTS + 8, LANES), F32),
+            pltpu.VMEM((4 * SLAB, 4 * SLAB), BF16),
+            pltpu.VMEM((3, 2 * RADIX, SLAB, POINTS), BF16),
             pltpu.VMEM((NGRID, 2 * NGRID), BF16),
             pltpu.VMEM((NGRID, 2 * NGRID), BF16),
             pltpu.VMEM(wide.shape, BF16),

time: 101 us -> 92.3 us (0.914)
  Pallas kernels: 33.6 us -> 24.9 us
    pallas_call x1, Pallas kernels: 33.6 us -> 24.9 us  [sample_power(): pl.pallas_call(sample_kernel, out_shape=jax.ShapeDtypeStruct((NGRID, NGRI...]
where the time goes in v5:
time: 92.3 us; the launch traced here: 91.8 us
  blocking collectives  32.2 us (35%)
  Pallas kernels  24.9 us (27%)
  waiting for transfers between devices  14.4 us (16%)
  starting transfers between devices  12.4 us (13%)
  other arithmetic  5.01 us (5%)
  local copies, waits for them, and re-layouts  2.79 us (3%)
    all_to_all x1, blocking collectives, per_device(): lax.all_to_all(power, 'row', split_axis=0, concat_axis=0, tiled=True)  32.2 us
    pallas_call x1, Pallas kernels, sample_power(): pl.pallas_call(sample_kernel, out_shape=jax.ShapeDtypeStruct((NGRID, NGRI...  24.9 us
    all_to_all x1, waiting for transfers between devices, per_device(): lax.all_to_all(lists, 'row', split_axis=0, concat_axis=0, tiled=True)  9.2 us
    all_to_all x1, starting transfers between devices, per_device(): lax.all_to_all(lists, 'row', split_axis=0, concat_axis=0, tiled=True)  8.13 us
    all_to_all x1, waiting for transfers between devices, per_device(): lax.all_to_all(mine, 'chan', split_axis=0, concat_axis=0, tiled=True)  5.18 us
    all_to_all x1, starting transfers between devices, per_device(): lax.all_to_all(mine, 'chan', split_axis=0, concat_axis=0, tiled=True)  4.31 us
    another operation x3, other arithmetic  2.51 us
  transfers between devices with their start and end apart: 2, of which 2 were waited for; matrix products, arithmetic and copies ran while one was open for 2% of the time, Pallas kernels for 0%

profile of v5, /device:TPU:0, one launch (start us, length us, event | category | flops | bytes accessed | tf_op | source)
XLA Modules:
  0.0 91.8 jit_solution(3629235355754379516)
XLA Ops:
  0.0 0.0 copy-start
  0.0 0.9 convert_reduce_fusion.2
  0.9 0.8 convert.20
  1.7 0.1 reshape.46
  1.8 0.1 stack.11
  2.0 0.8 select_convert_fusion
  2.8 0.1 reshape.45
  2.9 0.1 stack.10
  3.1 0.8 broadcast_in_dim.22
  3.8 8.1 %all-to-all-start = ((s16[16,3,32,128]{3,2,1,0:T(8,128)(2,1)}), s16[16,3,32,128]{3,2,1,0:T(8,128)(2,1)S(1)}, u32[]{:S(2)}, u32[]{:S(2)}) async-start(s16[16,3,32,128]{3,2,1,0:T(8,128)(2,1)} %broadcast_in_dim.22), calls=%async_computation | async-start | bytes 786432 | tf_op jit(solution)/shard_map/all_to_all | solution.py:327
  12.0 0.0 copy-done
  12.0 0.1 constant_dynamic-slice_fusion
  12.1 0.8 reshape.47
  12.9 9.2 %all-to-all-done.lists = s16[16,3,32,128]{3,2,1,0:T(8,128)(2,1)S(1)} async-done(((s16[16,3,32,128]{3,2,1,0:T(8,128)(2,1)}), s16[16,3,32,128]{3,2,1,0:T(8,128)(2,1)S(1)}, u32[]{:S(2)}, u32[]{:S(2)}) %all-to-all-start) | async-done | bytes 393248 | tf_op jit(solution)/shard_map/all_to_all | solution.py:327
  22.1 0.0 copy-start.1
  22.1 0.4 convert_reduce_fusion.1
  22.5 4.3 %all-to-all-start.1 = ((bf16[8,2,32,128]{3,2,1,0:T(8,128)(2,1)}), bf16[8,2,32,128]{3,2,1,0:T(8,128)(2,1)S(1)}, u32[]{:S(2)}, u32[]{:S(2)}) async-start(bf16[8,2,32,128]{3,2,1,0:T(8,128)(2,1)} %reshape.47), calls=%async_computation.1 | async-start | bytes 262144 | tf_op jit(solution)/shard_map/all_to_all | solution.py:331
  26.8 0.4 slice_reduce_fusion
  27.2 0.6 fusion.extent
  27.8 5.2 %all-to-all-done.1.volts = bf16[8,2,32,128]{3,2,1,0:T(8,128)(2,1)S(1)} async-done(((bf16[8,2,32,128]{3,2,1,0:T(8,128)(2,1)}), bf16[8,2,32,128]{3,2,1,0:T(8,128)(2,1)S(1)}, u32[]{:S(2)}, u32[]{:S(2)}) %all-to-all-start.1) | async-done | bytes 131104 | tf_op jit(solution)/shard_map/all_to_all | solution.py:331
  33.0 0.0 copy-start.2
  33.0 0.0 copy-done.1
  33.0 0.7 copy-done.2
  33.6 24.9 %shard_map.82 = bf16[1024,1024]{1,0:T(8,128)(2,1)} custom-call(f32[4,4]{1,0:T(4,128)} %bitcast.23, s32[16]{0:T(128)} %fusion.extent, bf16[8,2,32,128]{3,2,1,0:T(8,128)(2,1)} %copy-done.2, s16[16,3,32,128]{3,2,1,0:T(8,128)(2,1)} %copy-done.1, bf16[4,512,512]{2,1,0:T(8,128)(2,1)} %constant.42.clone.wide_from, bf16[4,512,512]{2,1,0:T(8,128)(2,1)} %constant.43.clone.tall_from), custom_call_target="tpu_custom_call" | custom-call | tf_op jit(solution)/shard_map/pallas_call | solution.py:278
  58.5 32.2 %all_to_all.15 = bf16[16,64,1024]{2,1,0:T(8,128)(2,1)S(1)} all-to-all(bf16[16,64,1024]{2,1,0:T(8,128)(2,1)} %bitcast.18), channel_id=1, replica_groups=mesh['chan'=8,'row'=16] {'row'}, dimensions={0} | all-to-all | bytes 4194304 | tf_op jit(solution)/shard_map/all_to_all | solution.py:342
  90.7 0.4 convert_reduce_fusion
  91.1 0.7 multiply_bitcast_fusion
  (6 shorter events, 0.1 us)
Async XLA Ops:
  0.0 12.0 %copy-start = (bf16[8,16,2,4096]{3,2,1,0:T(2,128)(2,1)S(1)}, bf16[8,16,2,4096]{3,2,1,0:T(2,128)(2,1)}, u32[]{:S(2)}) copy-start(bf16[8,16,2,4096]{3,2,1,0:T(2,128)(2,1)} %param.8) | copy-start | bytes 6291460
  3.8 18.2 %all-to-all-start = ((s16[16,3,32,128]{3,2,1,0:T(8,128)(2,1)}), s16[16,3,32,128]{3,2,1,0:T(8,128)(2,1)S(1)}, u32[]{:S(2)}, u32[]{:S(2)}) async-start(s16[16,3,32,128]{3,2,1,0:T(8,128)(2,1)} %broadcast_in_dim.22), calls=%async_computation | async-start | bytes 786432 | tf_op jit(solution)/shard_map/all_to_all | solution.py:327
  22.1 10.9 %copy-start.1 = (s16[16,3,32,128]{3,2,1,0:T(8,128)(2,1)}, s16[16,3,32,128]{3,2,1,0:T(8,128)(2,1)S(1)}, u32[]{:S(2)}) copy-start(s16[16,3,32,128]{3,2,1,0:T(8,128)(2,1)S(1)} %all-to-all-done.lists) | copy-start | bytes 1179652
  22.5 10.4 %all-to-all-start.1 = ((bf16[8,2,32,128]{3,2,1,0:T(8,128)(2,1)}), bf16[8,2,32,128]{3,2,1,0:T(8,128)(2,1)S(1)}, u32[]{:S(2)}, u32[]{:S(2)}) async-start(bf16[8,2,32,128]{3,2,1,0:T(8,128)(2,1)} %reshape.47), calls=%async_computation.1 | async-start | bytes 262144 | tf_op jit(solution)/shard_map/all_to_all | solution.py:331
  33.0 0.7 copy-start.2

commit v6 on v5

--- a/solution.py
+++ b/solution.py
@@ -46,8 +46,8 @@
 
 
 def sample_kernel(
-    taps, extent, volts, lists, wide_from, tall_from, power, slots, bands, cells, aperture,
-    spectrum, wide, tall, arrived,
+    taps, extent, volts, lists, wide_from, tall_from, power_to, slots, bands, cells, aperture,
+    spectrum, wide, tall, power, arrived, left_for,
 ):
     slabs = lists.shape[0]
     groups = volts.shape[0]
@@ -160,31 +160,32 @@
                 values[i] = jnp.where(hit, pick(row, member_lane), values[i])
         kind = (columns & (RADIX - 1)) + RADIX * (columns >> 9)
         point = ((columns >> 2) & (LANES - 1)).astype(F32)
-        planes = [
-            jnp.where(kind == half * RADIX + qx, values[i], 0.0)
-            for half in range(2)
-            for qx in range(RADIX)
-            for i in range(2)
-        ]
         cell = lax.broadcasted_iota(jnp.int32, (LANES, chunks * LANES), 0).astype(BF16)
         for qy in range(RADIX):
             placed = []
             for h in range(2):
                 at = [8 * c + 2 * qy + h for c in range(chunks)]
+                kinds = [
+                    jnp.where(
+                        own_row, jnp.broadcast_to(kind[a : a + 1, :], (8, LANES)), -1
+                    )
+                    for a in at
+                ]
+                spread = [
+                    [jnp.broadcast_to(v[a : a + 1, :], (8, LANES)) for a in at]
+                    for v in values
+                ]
                 left = jnp.concatenate(
                     [
                         jnp.concatenate(
                             [
-                                jnp.where(
-                                    own_row,
-                                    jnp.broadcast_to(plane[a : a + 1, :], (8, LANES)),
-                                    0.0,
-                                )
-                                for a in at
+                                jnp.where(kinds[c] == plane, spread[i][c], 0.0)
+                                for c in range(chunks)
                             ],
                             axis=1,
                         )
-                        for plane in planes
+                        for plane in range(2 * RADIX)
+                        for i in range(2)
                     ],
                     axis=0,
                 ).astype(BF16)
@@ -249,10 +250,14 @@
         return carry
 
     wide_copy.wait()
-    lax.fori_loop(0, RADIX, row_transform, 0)
+    lax.fori_loop(0, RADIX, row_transform, 0, unroll=True)
+
+    def hand_over(n):
+        rows = pl.ds(n * POINTS, POINTS)
+        return pltpu.make_async_copy(power.at[rows], power_to.at[rows], left_for.at[n])
 
     def column_transform(n, carry):
-        rows = pl.ds(pl.multiple_of(n * 256, 256), 256)
+        rows = pl.ds(n * POINTS, POINTS)
         parts = [
             jnp.dot(
                 spectrum[rows, 2 * q * POINTS : 2 * (q + 1) * POINTS],
@@ -271,7 +276,11 @@
         return carry
 
     tall_copy.wait()
-    lax.fori_loop(0, NGRID // 256, column_transform, 0)
+    for n in range(RADIX):
+        column_transform(n, 0)
+        hand_over(n).start()
+    for n in range(RADIX):
+        hand_over(n).wait()
 
 
 def sample_power(taps, extent, volts, lists, wide, tall):
@@ -281,7 +290,7 @@
         in_specs=[pl.BlockSpec(memory_space=pltpu.SMEM)] * 2
         + [pl.BlockSpec(memory_space=pltpu.VMEM)] * 2
         + [pl.BlockSpec(memory_space=pl.ANY)] * 2,
-        out_specs=pl.BlockSpec(memory_space=pltpu.VMEM),
+        out_specs=pl.BlockSpec(memory_space=pl.ANY),
         scratch_shapes=[
             pltpu.VMEM((2, lists.shape[0], 32, LANES), F32),
             pltpu.VMEM((4 * SLAB, 4 * SLAB), BF16),
@@ -290,7 +299,9 @@
             pltpu.VMEM((NGRID, 2 * NGRID), BF16),
             pltpu.VMEM(wide.shape, BF16),
             pltpu.VMEM(tall.shape, BF16),
+            pltpu.VMEM((NGRID, NGRID), BF16),
             pltpu.SemaphoreType.DMA((2,)),
+            pltpu.SemaphoreType.DMA((RADIX,)),
         ],
         compiler_params=pltpu.CompilerParams(vmem_limit_bytes=56 * 2**20),
     )(taps, extent, volts, lists, wide, tall)
@@ -327,7 +338,6 @@
     lists = lax.all_to_all(lists, "row", split_axis=0, concat_axis=0, tiled=True)
     mine = lax.dynamic_index_in_dim(voltages, lax.axis_index("row"), 1, keepdims=False)
     mine = mine.reshape(chan_count, 2, group_size // LANES, LANES)
-    lists, mine = lax.optimization_barrier((lists, mine))
     volts = lax.all_to_all(mine, "chan", split_axis=0, concat_axis=0, tiled=True)
     wide, tall = stage_tables()
     power = sample_power(

time: 92.3 us -> 90 us (0.975)
  Pallas kernels: 24.9 us -> 23.1 us
    pallas_call x1, Pallas kernels: 24.9 us -> 23.1 us  [sample_power(): pl.pallas_call(sample_kernel, out_shape=jax.ShapeDtypeStruct((NGRID, NGRI...]
  transfers between devices with their start and end apart: 2 -> 2, of which waited for: 2 -> 2; matrix products, arithmetic and copies ran while one was open for 2% -> 3% of each run, Pallas kernels for 0% -> 0%
where the time goes in v6:
time: 90 us; the launch traced here: 89.5 us
  blocking collectives  32.2 us (36%)
  Pallas kernels  23.1 us (26%)
  waiting for transfers between devices  13.9 us (15%)
  starting transfers between devices  12.4 us (14%)
  other arithmetic  5.01 us (6%)
  local copies, waits for them, and re-layouts  2.79 us (3%)
    all_to_all x1, blocking collectives, per_device(): lax.all_to_all(power, 'row', split_axis=0, concat_axis=0, tiled=True)  32.2 us
    pallas_call x1, Pallas kernels, sample_power(): pl.pallas_call(sample_kernel, out_shape=jax.ShapeDtypeStruct((NGRID, NGRI...  23.1 us
    all_to_all x1, waiting for transfers between devices, per_device(): lax.all_to_all(lists, 'row', split_axis=0, concat_axis=0, tiled=True)  9.2 us
    all_to_all x1, starting transfers between devices, per_device(): lax.all_to_all(lists, 'row', split_axis=0, concat_axis=0, tiled=True)  8.13 us
    all_to_all x1, waiting for transfers between devices, per_device(): lax.all_to_all(mine, 'chan', split_axis=0, concat_axis=0, tiled=True)  4.75 us
    all_to_all x1, starting transfers between devices, per_device(): lax.all_to_all(mine, 'chan', split_axis=0, concat_axis=0, tiled=True)  4.3 us
    another operation x3, other arithmetic  2.51 us
  transfers between devices with their start and end apart: 2, of which 2 were waited for; matrix products, arithmetic and copies ran while one was open for 3% of the time, Pallas kernels for 0%

profile of v6, /device:TPU:0, one launch (start us, length us, event | category | flops | bytes accessed | tf_op | source)
XLA Modules:
  0.0 89.5 jit_solution(4668890782219117064)
XLA Ops:
  0.0 0.0 copy-start
  0.0 0.9 %convert_reduce_fusion.2 = s16[8,512]{1,0:T(8,128)(2,1)S(1)} fusion(s32[8,1,512]{2,1,0:T(1,128)} %param.10), kind=kLoop, calls=%fused_computation.8 | loop fusion | flops 4096 | bytes 24576 | tf_op jit(solution)/shard_map/convert.11
  0.9 0.8 convert.20
  1.7 0.1 reshape.46
  1.8 0.1 stack.11
  2.0 0.8 select_convert_fusion
  2.8 0.1 reshape.45
  2.9 0.1 stack.10
  3.1 0.8 broadcast_in_dim.22
  3.8 8.1 %all-to-all-start = ((s16[16,3,32,128]{3,2,1,0:T(8,128)(2,1)}), s16[16,3,32,128]{3,2,1,0:T(8,128)(2,1)S(1)}, u32[]{:S(2)}, u32[]{:S(2)}) async-start(s16[16,3,32,128]{3,2,1,0:T(8,128)(2,1)} %broadcast_in_dim.22), calls=%async_computation | async-start | bytes 786432 | tf_op jit(solution)/shard_map/all_to_all | solution.py:338
  12.0 0.0 copy-done
  12.0 0.1 constant_dynamic-slice_fusion
  12.1 0.8 reshape.47
  12.9 9.2 %all-to-all-done.lists = s16[16,3,32,128]{3,2,1,0:T(8,128)(2,1)S(1)} async-done(((s16[16,3,32,128]{3,2,1,0:T(8,128)(2,1)}), s16[16,3,32,128]{3,2,1,0:T(8,128)(2,1)S(1)}, u32[]{:S(2)}, u32[]{:S(2)}) %all-to-all-start) | async-done | bytes 393248 | tf_op jit(solution)/shard_map/all_to_all | solution.py:338
  22.1 0.0 copy-start.1
  22.1 4.3 %all-to-all-start.1 = ((bf16[8,2,32,128]{3,2,1,0:T(8,128)(2,1)}), bf16[8,2,32,128]{3,2,1,0:T(8,128)(2,1)S(1)}, u32[]{:S(2)}, u32[]{:S(2)}) async-start(bf16[8,2,32,128]{3,2,1,0:T(8,128)(2,1)} %reshape.47), calls=%async_computation.1 | async-start | bytes 262144 | tf_op jit(solution)/shard_map/all_to_all | solution.py:341
  26.4 0.4 slice_reduce_fusion
  26.8 0.4 convert_reduce_fusion.1
  27.2 0.6 fusion.extent
  27.8 4.8 %all-to-all-done.1.volts = bf16[8,2,32,128]{3,2,1,0:T(8,128)(2,1)S(1)} async-done(((bf16[8,2,32,128]{3,2,1,0:T(8,128)(2,1)}), bf16[8,2,32,128]{3,2,1,0:T(8,128)(2,1)S(1)}, u32[]{:S(2)}, u32[]{:S(2)}) %all-to-all-start.1) | async-done | bytes 131104 | tf_op jit(solution)/shard_map/all_to_all | solution.py:341
  32.5 0.0 copy-start.2
  32.5 0.0 copy-done.1
  32.5 0.7 copy-done.2
  33.2 23.1 %shard_map.82 = bf16[1024,1024]{1,0:T(8,128)(2,1)} custom-call(f32[4,4]{1,0:T(4,128)} %bitcast.23, s32[16]{0:T(128)} %fusion.extent, bf16[8,2,32,128]{3,2,1,0:T(8,128)(2,1)} %copy-done.2, s16[16,3,32,128]{3,2,1,0:T(8,128)(2,1)} %copy-done.1, bf16[4,512,512]{2,1,0:T(8,128)(2,1)} %constant.42.clone.wide_from, bf16[4,512,512]{2,1,0:T(8,128)(2,1)} %constant.43.clone.tall_from), custom_call_target="tpu_custom_call" | custom-call | tf_op jit(solution)/shard_map/pallas_call | solution.py:287
  56.2 32.2 %all_to_all.15 = bf16[16,64,1024]{2,1,0:T(8,128)(2,1)S(1)} all-to-all(bf16[16,64,1024]{2,1,0:T(8,128)(2,1)} %bitcast.18), channel_id=1, replica_groups=mesh['chan'=8,'row'=16] {'row'}, dimensions={0} | all-to-all | bytes 4194304 | tf_op jit(solution)/shard_map/all_to_all | solution.py:352
  88.4 0.4 convert_reduce_fusion
  88.8 0.7 multiply_bitcast_fusion
  (6 shorter events, 0.1 us)
Async XLA Ops:
  0.0 12.0 %copy-start = (bf16[8,16,2,4096]{3,2,1,0:T(2,128)(2,1)S(1)}, bf16[8,16,2,4096]{3,2,1,0:T(2,128)(2,1)}, u32[]{:S(2)}) copy-start(bf16[8,16,2,4096]{3,2,1,0:T(2,128)(2,1)} %param.8) | copy-start | bytes 6291460
  3.8 18.2 %all-to-all-start = ((s16[16,3,32,128]{3,2,1,0:T(8,128)(2,1)}), s16[16,3,32,128]{3,2,1,0:T(8,128)(2,1)S(1)}, u32[]{:S(2)}, u32[]{:S(2)}) async-start(s16[16,3,32,128]{3,2,1,0:T(8,128)(2,1)} %broadcast_in_dim.22), calls=%async_computation | async-start | bytes 786432 | tf_op jit(solution)/shard_map/all_to_all | solution.py:338
  22.1 10.4 %copy-start.1 = (s16[16,3,32,128]{3,2,1,0:T(8,128)(2,1)}, s16[16,3,32,128]{3,2,1,0:T(8,128)(2,1)S(1)}, u32[]{:S(2)}) copy-start(s16[16,3,32,128]{3,2,1,0:T(8,128)(2,1)S(1)} %all-to-all-done.lists) | copy-start | bytes 1179652
  22.1 10.4 %all-to-all-start.1 = ((bf16[8,2,32,128]{3,2,1,0:T(8,128)(2,1)}), bf16[8,2,32,128]{3,2,1,0:T(8,128)(2,1)S(1)}, u32[]{:S(2)}, u32[]{:S(2)}) async-start(bf16[8,2,32,128]{3,2,1,0:T(8,128)(2,1)} %reshape.47), calls=%async_computation.1 | async-start | bytes 262144 | tf_op jit(solution)/shard_map/all_to_all | solution.py:341
  32.5 0.7 copy-start.2

commit v7 on v6

--- a/solution.py
+++ b/solution.py
@@ -333,12 +333,13 @@
     row_count = lax.axis_size("row")
     group_size = voltages.shape[3]
     samples = voltages.shape[1]
-    lists = slab_lists(route_lists, row_members, row_counts, anchor_cols)
-    lists = jnp.broadcast_to(lists[None], (row_count,) + lists.shape)
-    lists = lax.all_to_all(lists, "row", split_axis=0, concat_axis=0, tiled=True)
     mine = lax.dynamic_index_in_dim(voltages, lax.axis_index("row"), 1, keepdims=False)
     mine = mine.reshape(chan_count, 2, group_size // LANES, LANES)
     volts = lax.all_to_all(mine, "chan", split_axis=0, concat_axis=0, tiled=True)
+    lists = slab_lists(route_lists, row_members, row_counts, anchor_cols)
+    lists = jnp.broadcast_to(lists[None], (row_count,) + lists.shape)
+    volts, lists = lax.optimization_barrier((volts, lists))
+    lists = lax.all_to_all(lists, "row", split_axis=0, concat_axis=0, tiled=True)
     wide, tall = stage_tables()
     power = sample_power(
         kernel[0],

time: 90 us -> 88.4 us (0.982)
  blocking collectives: 32.2 us -> 49.3 us
  waiting for transfers between devices: 13.9 us -> 3.23 us
  starting transfers between devices: 12.4 us -> 4.38 us
    all_to_all x0 -> x1, blocking collectives: none -> 17.7 us  [per_device(): lax.all_to_all(lists, 'row', split_axis=0, concat_axis=0, tiled=True)]
    all_to_all x1 -> x0, waiting for transfers between devices: 9.2 us -> none  [per_device(): lax.all_to_all(lists, 'row', split_axis=0, concat_axis=0, tiled=True)]
    all_to_all x1 -> x0, starting transfers between devices: 8.13 us -> none  [per_device(): lax.all_to_all(lists, 'row', split_axis=0, concat_axis=0, tiled=True)]
    all_to_all x1, waiting for transfers between devices: 4.75 us -> 3.23 us  [per_device(): lax.all_to_all(mine, 'chan', split_axis=0, concat_axis=0, tiled=True)]
    unnamed x6, local copies, waits for them, and re-layouts: 0.66 us -> 1.6 us
  transfers between devices with their start and end apart: 2 -> 1, of which waited for: 2 -> 1; matrix products, arithmetic and copies ran while one was open for 3% -> 3% of each run, Pallas kernels for 0% -> 0%
where the time goes in v7:
time: 88.4 us; the launch traced here: 87.9 us
  blocking collectives  49.3 us (56%)
  Pallas kernels  23 us (26%)
  other arithmetic  4.86 us (5%)
  starting transfers between devices  4.38 us (5%)
  waiting for transfers between devices  3.23 us (4%)
  local copies, waits for them, and re-layouts  2.99 us (3%)
    all_to_all x1, blocking collectives, per_device(): lax.all_to_all(power, 'row', split_axis=0, concat_axis=0, tiled=True)  31.6 us
    pallas_call x1, Pallas kernels, sample_power(): pl.pallas_call(sample_kernel, out_shape=jax.ShapeDtypeStruct((NGRID, NGRI...  23 us
    all_to_all x1, blocking collectives, per_device(): lax.all_to_all(lists, 'row', split_axis=0, concat_axis=0, tiled=True)  17.7 us
    all_to_all x1, starting transfers between devices, per_device(): lax.all_to_all(mine, 'chan', split_axis=0, concat_axis=0, tiled=True)  4.38 us
    all_to_all x1, waiting for transfers between devices, per_device(): lax.all_to_all(mine, 'chan', split_axis=0, concat_axis=0, tiled=True)  3.23 us
    another operation x3, other arithmetic  2.36 us
  transfers between devices with their start and end apart: 1, of which 1 were waited for; matrix products, arithmetic and copies ran while one was open for 3% of the time, Pallas kernels for 0%

profile of v7, /device:TPU:0, one launch (start us, length us, event | category | flops | bytes accessed | tf_op | source)
XLA Modules:
  0.0 87.9 jit_solution(10128693306331055125)
XLA Ops:
  0.0 0.0 copy-start
  0.0 1.6 %copy-done = bf16[8,16,2,4096]{3,2,1,0:T(2,128)(2,1)S(1)} copy-done((bf16[8,16,2,4096]{3,2,1,0:T(2,128)(2,1)S(1)}, bf16[8,16,2,4096]{3,2,1,0:T(2,128)(2,1)}, u32[]{:S(2)}) %copy-start) | copy-done | bytes 2097176
  1.6 0.1 constant_dynamic-slice_fusion
  1.7 0.8 reshape.45
  2.5 4.4 %all-to-all-start = ((bf16[8,2,32,128]{3,2,1,0:T(8,128)(2,1)}), bf16[8,2,32,128]{3,2,1,0:T(8,128)(2,1)S(1)}, u32[]{:S(2)}, u32[]{:S(2)}) async-start(bf16[8,2,32,128]{3,2,1,0:T(8,128)(2,1)} %reshape.45), calls=%async_computation | async-start | bytes 262144 | tf_op jit(solution)/shard_map/all_to_all | solution.py:338
  6.8 0.8 select_convert_fusion
  7.7 0.8 convert_reduce_fusion.2
  8.5 0.8 convert.20
  9.2 0.1 reshape.47
  9.4 0.1 stack.11
  9.5 0.1 reshape.46
  9.6 0.1 stack.10
  9.7 3.2 %all-to-all-done.volts = bf16[8,2,32,128]{3,2,1,0:T(8,128)(2,1)S(1)} async-done(((bf16[8,2,32,128]{3,2,1,0:T(8,128)(2,1)}), bf16[8,2,32,128]{3,2,1,0:T(8,128)(2,1)S(1)}, u32[]{:S(2)}, u32[]{:S(2)}) %all-to-all-start) | async-done | bytes 131104 | tf_op jit(solution)/shard_map/all_to_all | solution.py:338
  13.0 0.0 copy-start.2
  13.0 0.1 broadcast_in_dim.22
  13.0 17.7 %all_to_all.15.lists = s16[16,3,32,128]{3,2,1,0:T(8,128)(2,1)S(1)} all-to-all(s16[16,3,32,128]{3,2,1,0:T(8,128)(2,1)S(1)} %broadcast_in_dim.22), channel_id=1, replica_groups=mesh['chan'=8,'row'=16] {'row'}, dimensions={0} | all-to-all | bytes 786432 | tf_op jit(solution)/shard_map/all_to_all | solution.py:342
  30.8 0.0 copy-start.1
  30.8 0.4 slice_reduce_fusion
  31.2 0.4 convert_reduce_fusion.1
  31.6 0.6 fusion.extent
  32.2 0.0 copy-done.2
  32.2 0.0 copy-done.1
  32.2 23.0 %shard_map.82 = bf16[1024,1024]{1,0:T(8,128)(2,1)} custom-call(f32[4,4]{1,0:T(4,128)} %bitcast.23, s32[16]{0:T(128)} %fusion.extent, bf16[8,2,32,128]{3,2,1,0:T(8,128)(2,1)} %copy-done.2, s16[16,3,32,128]{3,2,1,0:T(8,128)(2,1)} %copy-done.1, bf16[4,512,512]{2,1,0:T(8,128)(2,1)} %constant.42.clone.wide_from, bf16[4,512,512]{2,1,0:T(8,128)(2,1)} %constant.43.clone.tall_from), custom_call_target="tpu_custom_call" | custom-call | tf_op jit(solution)/shard_map/pallas_call | solution.py:287
  55.2 31.6 %all_to_all.16 = bf16[16,64,1024]{2,1,0:T(8,128)(2,1)S(1)} all-to-all(bf16[16,64,1024]{2,1,0:T(8,128)(2,1)} %bitcast.18), channel_id=1, replica_groups=mesh['chan'=8,'row'=16] {'row'}, dimensions={0} | all-to-all | bytes 4194304 | tf_op jit(solution)/shard_map/all_to_all | solution.py:353
  86.8 0.4 convert_reduce_fusion
  87.2 0.7 multiply_bitcast_fusion
  (6 shorter events, 0.1 us)
Async XLA Ops:
  0.0 1.6 %copy-start = (bf16[8,16,2,4096]{3,2,1,0:T(2,128)(2,1)S(1)}, bf16[8,16,2,4096]{3,2,1,0:T(2,128)(2,1)}, u32[]{:S(2)}) copy-start(bf16[8,16,2,4096]{3,2,1,0:T(2,128)(2,1)} %param.8) | copy-start | bytes 6291460
  2.5 10.5 %all-to-all-start = ((bf16[8,2,32,128]{3,2,1,0:T(8,128)(2,1)}), bf16[8,2,32,128]{3,2,1,0:T(8,128)(2,1)S(1)}, u32[]{:S(2)}, u32[]{:S(2)}) async-start(bf16[8,2,32,128]{3,2,1,0:T(8,128)(2,1)} %reshape.45), calls=%async_computation | async-start | bytes 262144 | tf_op jit(solution)/shard_map/all_to_all | solution.py:338
  13.0 19.2 %copy-start.2 = (bf16[8,2,32,128]{3,2,1,0:T(8,128)(2,1)}, bf16[8,2,32,128]{3,2,1,0:T(8,128)(2,1)S(1)}, u32[]{:S(2)}) copy-start(bf16[8,2,32,128]{3,2,1,0:T(8,128)(2,1)S(1)} %all-to-all-done.volts) | copy-start | bytes 393220
  30.8 1.4 %copy-start.1 = (s16[16,3,32,128]{3,2,1,0:T(8,128)(2,1)}, s16[16,3,32,128]{3,2,1,0:T(8,128)(2,1)S(1)}, u32[]{:S(2)}) copy-start(s16[16,3,32,128]{3,2,1,0:T(8,128)(2,1)S(1)} %all_to_all.15.lists) | copy-start | bytes 1179652

commit v8 on v7

--- a/solution.py
+++ b/solution.py
@@ -83,7 +83,7 @@
     def gather_pair(pair, carry):
         first, second = 2 * pair, 2 * pair + 1
         routes = [lists[r, 0].astype(jnp.int32) for r in (first, second)]
-        last = jnp.maximum(extent[first] & 3, extent[second] & 3)
+        last = jnp.maximum(extent[first], extent[second])
         for s in range(4):
 
             @pl.when(last >= s)
@@ -212,11 +212,11 @@
                     )
 
     def grid_slab(r, carry):
-        @pl.when(extent[r] < 4)
+        @pl.when(extent[r] < 2)
         def _():
             grid_chunks(r, 2, 16)
 
-        @pl.when(extent[r] >= 4)
+        @pl.when(extent[r] >= 2)
         def _():
             grid_chunks(r, 4, 32)
 
@@ -322,10 +322,9 @@
 
 def list_extents(lists):
     slot = lists[:, 1].astype(jnp.int32)
-    top = jnp.max(slot, axis=(1, 2))
-    late = jnp.max(slot[:, 16:], axis=(1, 2))
-    wide = (top >= 2048) | (late >= 0)
-    return (jnp.maximum(top, 0) >> 10) + jnp.where(wide, 4, 0)
+    late = jnp.arange(slot.shape[1], dtype=jnp.int32)[None, :, None] >= 16
+    code = jnp.where(slot < 0, 0, (slot >> 10) + jnp.where(late, 8, 0))
+    return jnp.max(code, axis=(1, 2))
 
 
 def per_device(voltages, kernel, route_lists, row_members, row_counts, anchor_cols):

time: 88.4 us -> 89.2 us (level)
  blocking collectives: 49.3 us -> 31.5 us
  waiting for transfers between devices: 3.23 us -> 13.1 us
  starting transfers between devices: 4.38 us -> 12.4 us
    all_to_all x1 -> x0, blocking collectives: 17.7 us -> none  [per_device(): lax.all_to_all(lists, 'row', split_axis=0, concat_axis=0, tiled=True)]
    all_to_all x0 -> x1, waiting for transfers between devices: none -> 9.88 us  [per_device(): lax.all_to_all(lists, 'row', split_axis=0, concat_axis=0, tiled=True)]
    all_to_all x0 -> x1, starting transfers between devices: none -> 8.05 us  [per_device(): lax.all_to_all(lists, 'row', split_axis=0, concat_axis=0, tiled=True)]
  transfers between devices with their start and end apart: 1 -> 2, of which waited for: 1 -> 2; matrix products, arithmetic and copies ran while one was open for 3% -> 3% of each run, Pallas kernels for 0% -> 0%
where the time goes in v8:
time: 89.2 us; the launch traced here: 88.6 us
  blocking collectives  31.5 us (35%)
  Pallas kernels  23.2 us (26%)
  waiting for transfers between devices  13.1 us (15%)
  starting transfers between devices  12.4 us (14%)
  other arithmetic  4.52 us (5%)
  local copies, waits for them, and re-layouts  3.73 us (4%)
    all_to_all x1, blocking collectives, per_device(): lax.all_to_all(power, 'row', split_axis=0, concat_axis=0, tiled=True)  31.5 us
    pallas_call x1, Pallas kernels, sample_power(): pl.pallas_call(sample_kernel, out_shape=jax.ShapeDtypeStruct((NGRID, NGRI...  23.2 us
    all_to_all x1, waiting for transfers between devices, per_device(): lax.all_to_all(lists, 'row', split_axis=0, concat_axis=0, tiled=True)  9.88 us
    all_to_all x1, starting transfers between devices, per_device(): lax.all_to_all(lists, 'row', split_axis=0, concat_axis=0, tiled=True)  8.05 us
    all_to_all x1, starting transfers between devices, per_device(): lax.all_to_all(mine, 'chan', split_axis=0, concat_axis=0, tiled=True)  4.38 us
    all_to_all x1, waiting for transfers between devices, per_device(): lax.all_to_all(mine, 'chan', split_axis=0, concat_axis=0, tiled=True)  3.23 us
    another operation x3, other arithmetic  2.36 us
  transfers between devices with their start and end apart: 2, of which 2 were waited for; matrix products, arithmetic and copies ran while one was open for 3% of the time, Pallas kernels for 0%

profile of v8, /device:TPU:0, one launch (start us, length us, event | category | flops | bytes accessed | tf_op | source)
XLA Modules:
  0.0 88.6 jit_solution(10169581976108757412)
XLA Ops:
  0.0 0.0 copy-start
  0.0 1.6 %copy-done = bf16[8,16,2,4096]{3,2,1,0:T(2,128)(2,1)S(1)} copy-done((bf16[8,16,2,4096]{3,2,1,0:T(2,128)(2,1)S(1)}, bf16[8,16,2,4096]{3,2,1,0:T(2,128)(2,1)}, u32[]{:S(2)}) %copy-start) | copy-done | bytes 2097176
  1.6 0.1 constant_dynamic-slice_fusion
  1.7 0.8 reshape.56
  2.5 4.4 %all-to-all-start = ((bf16[8,2,32,128]{3,2,1,0:T(8,128)(2,1)}), bf16[8,2,32,128]{3,2,1,0:T(8,128)(2,1)S(1)}, u32[]{:S(2)}, u32[]{:S(2)}) async-start(bf16[8,2,32,128]{3,2,1,0:T(8,128)(2,1)} %reshape.56), calls=%async_computation | async-start | bytes 262144 | tf_op jit(solution)/shard_map/all_to_all | solution.py:337
  6.8 0.8 select_convert_fusion
  7.7 0.8 convert_reduce_fusion.1
  8.5 0.8 convert.20
  9.2 0.1 reshape.58
  9.4 0.1 stack.11
  9.5 0.1 reshape.57
  9.6 0.1 stack.10
  9.7 3.2 %all-to-all-done.volts = bf16[8,2,32,128]{3,2,1,0:T(8,128)(2,1)S(1)} async-done(((bf16[8,2,32,128]{3,2,1,0:T(8,128)(2,1)}), bf16[8,2,32,128]{3,2,1,0:T(8,128)(2,1)S(1)}, u32[]{:S(2)}, u32[]{:S(2)}) %all-to-all-start) | async-done | bytes 131104 | tf_op jit(solution)/shard_map/all_to_all | solution.py:337
  13.0 0.0 copy-start.2
  13.0 0.8 broadcast_in_dim.27
  13.8 8.0 %all-to-all-start.1 = ((s16[16,3,32,128]{3,2,1,0:T(8,128)(2,1)}), s16[16,3,32,128]{3,2,1,0:T(8,128)(2,1)S(1)}, u32[]{:S(2)}, u32[]{:S(2)}) async-start(s16[16,3,32,128]{3,2,1,0:T(8,128)(2,1)} %broadcast_in_dim.27), calls=%async_computation.1 | async-start | bytes 786432 | tf_op jit(solution)/shard_map/all_to_all | solution.py:341
  21.8 9.9 %all-to-all-done.1.lists = s16[16,3,32,128]{3,2,1,0:T(8,128)(2,1)S(1)} async-done(((s16[16,3,32,128]{3,2,1,0:T(8,128)(2,1)}), s16[16,3,32,128]{3,2,1,0:T(8,128)(2,1)S(1)}, u32[]{:S(2)}, u32[]{:S(2)}) %all-to-all-start.1) | async-done | bytes 393248 | tf_op jit(solution)/shard_map/all_to_all | solution.py:341
  31.7 0.0 copy-start.1
  31.7 1.0 %fusion.4.extent = s32[16]{0:T(128)} fusion(s16[16,3,32,128]{3,2,1,0:T(8,128)(2,1)S(1)} %all-to-all-done.1.lists, s32[32]{0:T(128)S(1)} %compare_select_fusion), kind=kLoop, calls=%fused_computation.7 | loop fusion | flops 393200 | bytes 131264 | tf_op jit(solution)/shard_map/reduce_max | solution.py:327
  32.8 0.0 copy-done.2
  32.8 0.0 copy-done.1
  32.8 23.2 %shard_map.82 = bf16[1024,1024]{1,0:T(8,128)(2,1)} custom-call(f32[4,4]{1,0:T(4,128)} %bitcast.41, s32[16]{0:T(128)} %fusion.4.extent, bf16[8,2,32,128]{3,2,1,0:T(8,128)(2,1)} %copy-done.2, s16[16,3,32,128]{3,2,1,0:T(8,128)(2,1)} %copy-done.1, bf16[4,512,512]{2,1,0:T(8,128)(2,1)} %constant.16.clone.wide_from, bf16[4,512,512]{2,1,0:T(8,128)(2,1)} %constant.42.clone.tall_from), custom_call_target="tpu_custom_call" | custom-call | tf_op jit(solution)/shard_map/pallas_call | solution.py:287
  56.0 31.5 %all_to_all.15 = bf16[16,64,1024]{2,1,0:T(8,128)(2,1)S(1)} all-to-all(bf16[16,64,1024]{2,1,0:T(8,128)(2,1)} %bitcast.36), channel_id=1, replica_groups=mesh['chan'=8,'row'=16] {'row'}, dimensions={0} | all-to-all | bytes 4194304 | tf_op jit(solution)/shard_map/all_to_all | solution.py:352
  87.5 0.4 convert_reduce_fusion
  87.9 0.7 multiply_bitcast_fusion
  (6 shorter events, 0.1 us)
Async XLA Ops:
  0.0 1.6 %copy-start = (bf16[8,16,2,4096]{3,2,1,0:T(2,128)(2,1)S(1)}, bf16[8,16,2,4096]{3,2,1,0:T(2,128)(2,1)}, u32[]{:S(2)}) copy-start(bf16[8,16,2,4096]{3,2,1,0:T(2,128)(2,1)} %param.8) | copy-start | bytes 6291460
  2.5 10.5 %all-to-all-start = ((bf16[8,2,32,128]{3,2,1,0:T(8,128)(2,1)}), bf16[8,2,32,128]{3,2,1,0:T(8,128)(2,1)S(1)}, u32[]{:S(2)}, u32[]{:S(2)}) async-start(bf16[8,2,32,128]{3,2,1,0:T(8,128)(2,1)} %reshape.56), calls=%async_computation | async-start | bytes 262144 | tf_op jit(solution)/shard_map/all_to_all | solution.py:337
  13.0 19.8 %copy-start.2 = (bf16[8,2,32,128]{3,2,1,0:T(8,128)(2,1)}, bf16[8,2,32,128]{3,2,1,0:T(8,128)(2,1)S(1)}, u32[]{:S(2)}) copy-start(bf16[8,2,32,128]{3,2,1,0:T(8,128)(2,1)S(1)} %all-to-all-done.volts) | copy-start | bytes 393220
  13.8 18.0 %all-to-all-start.1 = ((s16[16,3,32,128]{3,2,1,0:T(8,128)(2,1)}), s16[16,3,32,128]{3,2,1,0:T(8,128)(2,1)S(1)}, u32[]{:S(2)}, u32[]{:S(2)}) async-start(s16[16,3,32,128]{3,2,1,0:T(8,128)(2,1)} %broadcast_in_dim.27), calls=%async_computation.1 | async-start | bytes 786432 | tf_op jit(solution)/shard_map/all_to_all | solution.py:341
  31.7 1.0 %copy-start.1 = (s16[16,3,32,128]{3,2,1,0:T(8,128)(2,1)}, s16[16,3,32,128]{3,2,1,0:T(8,128)(2,1)S(1)}, u32[]{:S(2)}) copy-start(s16[16,3,32,128]{3,2,1,0:T(8,128)(2,1)S(1)} %all-to-all-done.1.lists) | copy-start | bytes 1179652

commit v9 on v7

--- a/solution.py
+++ b/solution.py
@@ -84,17 +84,17 @@
         first, second = 2 * pair, 2 * pair + 1
         routes = [lists[r, 0].astype(jnp.int32) for r in (first, second)]
         last = jnp.maximum(extent[first] & 3, extent[second] & 3)
-        for s in range(4):
+        for s in (0, 2):
 
             @pl.when(last >= s)
             def _():
-                for g in range(groups):
+                for g in range(2 * groups):
                     k = 8 * s + g
                     route = jnp.concatenate([a[k : k + 1, :] for a in routes], axis=1)
                     lane_spot = (route & (LANES - 1)).astype(F32).astype(BF16)
                     onehot = jnp.where(lane_of == lane_spot, BF16(1), BF16(0))
                     rows = jnp.dot(
-                        volts[g].reshape(64, LANES),
+                        volts[g % groups].reshape(64, LANES),
                         onehot,
                         preferred_element_type=F32,
                     )

time: 88.4 us -> 87 us (0.984)
  Pallas kernels: 23 us -> 21.6 us
    pallas_call x1, Pallas kernels: 23 us -> 21.6 us  [sample_power(): pl.pallas_call(sample_kernel, out_shape=jax.ShapeDtypeStruct((NGRID, NGRI...]
where the time goes in v9:
time: 87 us; the launch traced here: 86.4 us
  blocking collectives  49.3 us (57%)
  Pallas kernels  21.6 us (25%)
  other arithmetic  4.86 us (6%)
  starting transfers between devices  4.38 us (5%)
  waiting for transfers between devices  3.23 us (4%)
  local copies, waits for them, and re-layouts  2.99 us (3%)
    all_to_all x1, blocking collectives, per_device(): lax.all_to_all(power, 'row', split_axis=0, concat_axis=0, tiled=True)  31.5 us
    pallas_call x1, Pallas kernels, sample_power(): pl.pallas_call(sample_kernel, out_shape=jax.ShapeDtypeStruct((NGRID, NGRI...  21.6 us
    all_to_all x1, blocking collectives, per_device(): lax.all_to_all(lists, 'row', split_axis=0, concat_axis=0, tiled=True)  17.7 us
    all_to_all x1, starting transfers between devices, per_device(): lax.all_to_all(mine, 'chan', split_axis=0, concat_axis=0, tiled=True)  4.38 us
    all_to_all x1, waiting for transfers between devices, per_device(): lax.all_to_all(mine, 'chan', split_axis=0, concat_axis=0, tiled=True)  3.23 us
    another operation x3, other arithmetic  2.36 us
  transfers between devices with their start and end apart: 1, of which 1 were waited for; matrix products, arithmetic and copies ran while one was open for 3% of the time, Pallas kernels for 0%

profile of v9, /device:TPU:0, one launch (start us, length us, event | category | flops | bytes accessed | tf_op | source)
XLA Modules:
  0.0 86.4 jit_solution(6423465225424025808)
XLA Ops:
  0.0 0.0 copy-start
  0.0 1.6 %copy-done = bf16[8,16,2,4096]{3,2,1,0:T(2,128)(2,1)S(1)} copy-done((bf16[8,16,2,4096]{3,2,1,0:T(2,128)(2,1)S(1)}, bf16[8,16,2,4096]{3,2,1,0:T(2,128)(2,1)}, u32[]{:S(2)}) %copy-start) | copy-done | bytes 2097176
  1.6 0.1 constant_dynamic-slice_fusion
  1.7 0.8 reshape.45
  2.5 4.4 %all-to-all-start = ((bf16[8,2,32,128]{3,2,1,0:T(8,128)(2,1)}), bf16[8,2,32,128]{3,2,1,0:T(8,128)(2,1)S(1)}, u32[]{:S(2)}, u32[]{:S(2)}) async-start(bf16[8,2,32,128]{3,2,1,0:T(8,128)(2,1)} %reshape.45), calls=%async_computation | async-start | bytes 262144 | tf_op jit(solution)/shard_map/all_to_all | solution.py:338
  6.8 0.8 select_convert_fusion
  7.7 0.8 convert_reduce_fusion.2
  8.5 0.8 convert.20
  9.2 0.1 reshape.47
  9.4 0.1 stack.11
  9.5 0.1 reshape.46
  9.6 0.1 stack.10
  9.7 3.2 %all-to-all-done.volts = bf16[8,2,32,128]{3,2,1,0:T(8,128)(2,1)S(1)} async-done(((bf16[8,2,32,128]{3,2,1,0:T(8,128)(2,1)}), bf16[8,2,32,128]{3,2,1,0:T(8,128)(2,1)S(1)}, u32[]{:S(2)}, u32[]{:S(2)}) %all-to-all-start) | async-done | bytes 131104 | tf_op jit(solution)/shard_map/all_to_all | solution.py:338
  13.0 0.0 copy-start.2
  13.0 0.1 broadcast_in_dim.22
  13.0 17.7 %all_to_all.15.lists = s16[16,3,32,128]{3,2,1,0:T(8,128)(2,1)S(1)} all-to-all(s16[16,3,32,128]{3,2,1,0:T(8,128)(2,1)S(1)} %broadcast_in_dim.22), channel_id=1, replica_groups=mesh['chan'=8,'row'=16] {'row'}, dimensions={0} | all-to-all | bytes 786432 | tf_op jit(solution)/shard_map/all_to_all | solution.py:342
  30.8 0.0 copy-start.1
  30.8 0.4 slice_reduce_fusion
  31.2 0.4 convert_reduce_fusion.1
  31.6 0.6 fusion.extent
  32.2 0.0 copy-done.2
  32.2 0.0 copy-done.1
  32.2 21.6 %shard_map.82 = bf16[1024,1024]{1,0:T(8,128)(2,1)} custom-call(f32[4,4]{1,0:T(4,128)} %bitcast.23, s32[16]{0:T(128)} %fusion.extent, bf16[8,2,32,128]{3,2,1,0:T(8,128)(2,1)} %copy-done.2, s16[16,3,32,128]{3,2,1,0:T(8,128)(2,1)} %copy-done.1, bf16[4,512,512]{2,1,0:T(8,128)(2,1)} %constant.42.clone.wide_from, bf16[4,512,512]{2,1,0:T(8,128)(2,1)} %constant.43.clone.tall_from), custom_call_target="tpu_custom_call" | custom-call | tf_op jit(solution)/shard_map/pallas_call | solution.py:287
  53.8 31.5 %all_to_all.16 = bf16[16,64,1024]{2,1,0:T(8,128)(2,1)S(1)} all-to-all(bf16[16,64,1024]{2,1,0:T(8,128)(2,1)} %bitcast.18), channel_id=1, replica_groups=mesh['chan'=8,'row'=16] {'row'}, dimensions={0} | all-to-all | bytes 4194304 | tf_op jit(solution)/shard_map/all_to_all | solution.py:353
  85.3 0.4 convert_reduce_fusion
  85.7 0.7 multiply_bitcast_fusion
  (6 shorter events, 0.1 us)
Async XLA Ops:
  0.0 1.6 %copy-start = (bf16[8,16,2,4096]{3,2,1,0:T(2,128)(2,1)S(1)}, bf16[8,16,2,4096]{3,2,1,0:T(2,128)(2,1)}, u32[]{:S(2)}) copy-start(bf16[8,16,2,4096]{3,2,1,0:T(2,128)(2,1)} %param.8) | copy-start | bytes 6291460
  2.5 10.5 %all-to-all-start = ((bf16[8,2,32,128]{3,2,1,0:T(8,128)(2,1)}), bf16[8,2,32,128]{3,2,1,0:T(8,128)(2,1)S(1)}, u32[]{:S(2)}, u32[]{:S(2)}) async-start(bf16[8,2,32,128]{3,2,1,0:T(8,128)(2,1)} %reshape.45), calls=%async_computation | async-start | bytes 262144 | tf_op jit(solution)/shard_map/all_to_all | solution.py:338
  13.0 19.2 %copy-start.2 = (bf16[8,2,32,128]{3,2,1,0:T(8,128)(2,1)}, bf16[8,2,32,128]{3,2,1,0:T(8,128)(2,1)S(1)}, u32[]{:S(2)}) copy-start(bf16[8,2,32,128]{3,2,1,0:T(8,128)(2,1)S(1)} %all-to-all-done.volts) | copy-start | bytes 393220
  30.8 1.4 %copy-start.1 = (s16[16,3,32,128]{3,2,1,0:T(8,128)(2,1)}, s16[16,3,32,128]{3,2,1,0:T(8,128)(2,1)S(1)}, u32[]{:S(2)}) copy-start(s16[16,3,32,128]{3,2,1,0:T(8,128)(2,1)S(1)} %all_to_all.15.lists) | copy-start | bytes 1179652

commit v10 on v9

--- a/solution.py
+++ b/solution.py
@@ -80,14 +80,13 @@
     row_of = lax.broadcasted_iota(jnp.int32, (32, 2 * LANES), 0)
     lane_of = lax.broadcasted_iota(jnp.int32, (LANES, 2 * LANES), 0).astype(BF16)
 
-    def gather_pair(pair, carry):
+    def gather_pair(pair, carry, s):
         first, second = 2 * pair, 2 * pair + 1
         routes = [lists[r, 0].astype(jnp.int32) for r in (first, second)]
         last = jnp.maximum(extent[first] & 3, extent[second] & 3)
-        for s in (0, 2):
-
-            @pl.when(last >= s)
-            def _():
+        if True:
+
+            def look_up():
                 for g in range(2 * groups):
                     k = 8 * s + g
                     route = jnp.concatenate([a[k : k + 1, :] for a in routes], axis=1)
@@ -108,9 +107,14 @@
                         slots[i, first, k : k + 1, :] = entry[:, :LANES]
                         slots[i, second, k : k + 1, :] = entry[:, LANES:]
 
+        if s == 0:
+            look_up()
+        else:
+            pl.when(last >= s)(look_up)
         return carry
 
-    lax.fori_loop(0, slabs // 2, gather_pair, 0)
+    lax.fori_loop(0, slabs // 2, lambda n, c: gather_pair(n, c, 0), 0, unroll=2)
+    lax.fori_loop(0, slabs // 2, lambda n, c: gather_pair(n, c, 2), 0)
 
     def convolve(r):
         here = lax.rem(r + 3, 3)

time: 87 us -> 86.7 us (level)
  no operation moved by 1% of the time
where the time goes in v10:
time: 86.7 us; the launch traced here: 86.2 us
  blocking collectives  49.3 us (57%)
  Pallas kernels  21.3 us (25%)
  other arithmetic  4.86 us (6%)
  starting transfers between devices  4.38 us (5%)
  waiting for transfers between devices  3.23 us (4%)
  local copies, waits for them, and re-layouts  2.99 us (3%)
    all_to_all x1, blocking collectives, per_device(): lax.all_to_all(power, 'row', split_axis=0, concat_axis=0, tiled=True)  31.6 us
    pallas_call x1, Pallas kernels, sample_power(): pl.pallas_call(sample_kernel, out_shape=jax.ShapeDtypeStruct((NGRID, NGRI...  21.3 us
    all_to_all x1, blocking collectives, per_device(): lax.all_to_all(lists, 'row', split_axis=0, concat_axis=0, tiled=True)  17.7 us
    all_to_all x1, starting transfers between devices, per_device(): lax.all_to_all(mine, 'chan', split_axis=0, concat_axis=0, tiled=True)  4.38 us
    all_to_all x1, waiting for transfers between devices, per_device(): lax.all_to_all(mine, 'chan', split_axis=0, concat_axis=0, tiled=True)  3.23 us
    another operation x3, other arithmetic  2.36 us
  transfers between devices with their start and end apart: 1, of which 1 were waited for; matrix products, arithmetic and copies ran while one was open for 3% of the time, Pallas kernels for 0%

profile of v10, /device:TPU:0, one launch (start us, length us, event | category | flops | bytes accessed | tf_op | source)
XLA Modules:
  0.0 86.2 jit_solution(15629301747565107924)
XLA Ops:
  0.0 0.0 copy-start
  0.0 1.6 %copy-done = bf16[8,16,2,4096]{3,2,1,0:T(2,128)(2,1)S(1)} copy-done((bf16[8,16,2,4096]{3,2,1,0:T(2,128)(2,1)S(1)}, bf16[8,16,2,4096]{3,2,1,0:T(2,128)(2,1)}, u32[]{:S(2)}) %copy-start) | copy-done | bytes 2097176
  1.6 0.1 constant_dynamic-slice_fusion
  1.7 0.8 reshape.45
  2.5 4.4 %all-to-all-start = ((bf16[8,2,32,128]{3,2,1,0:T(8,128)(2,1)}), bf16[8,2,32,128]{3,2,1,0:T(8,128)(2,1)S(1)}, u32[]{:S(2)}, u32[]{:S(2)}) async-start(bf16[8,2,32,128]{3,2,1,0:T(8,128)(2,1)} %reshape.45), calls=%async_computation | async-start | bytes 262144 | tf_op jit(solution)/shard_map/all_to_all | solution.py:342
  6.8 0.8 select_convert_fusion
  7.7 0.8 convert_reduce_fusion.2
  8.5 0.8 convert.20
  9.2 0.1 reshape.47
  9.4 0.1 stack.11
  9.5 0.1 reshape.46
  9.6 0.1 stack.10
  9.7 3.2 %all-to-all-done.volts = bf16[8,2,32,128]{3,2,1,0:T(8,128)(2,1)S(1)} async-done(((bf16[8,2,32,128]{3,2,1,0:T(8,128)(2,1)}), bf16[8,2,32,128]{3,2,1,0:T(8,128)(2,1)S(1)}, u32[]{:S(2)}, u32[]{:S(2)}) %all-to-all-start) | async-done | bytes 131104 | tf_op jit(solution)/shard_map/all_to_all | solution.py:342
  13.0 0.0 copy-start.2
  13.0 0.1 broadcast_in_dim.22
  13.0 17.7 %all_to_all.15.lists = s16[16,3,32,128]{3,2,1,0:T(8,128)(2,1)S(1)} all-to-all(s16[16,3,32,128]{3,2,1,0:T(8,128)(2,1)S(1)} %broadcast_in_dim.22), channel_id=1, replica_groups=mesh['chan'=8,'row'=16] {'row'}, dimensions={0} | all-to-all | bytes 786432 | tf_op jit(solution)/shard_map/all_to_all | solution.py:346
  30.8 0.0 copy-start.1
  30.8 0.4 slice_reduce_fusion
  31.2 0.4 convert_reduce_fusion.1
  31.6 0.6 fusion.extent
  32.2 0.0 copy-done.2
  32.2 0.0 copy-done.1
  32.2 21.3 %shard_map.82 = bf16[1024,1024]{1,0:T(8,128)(2,1)} custom-call(f32[4,4]{1,0:T(4,128)} %bitcast.23, s32[16]{0:T(128)} %fusion.extent, bf16[8,2,32,128]{3,2,1,0:T(8,128)(2,1)} %copy-done.2, s16[16,3,32,128]{3,2,1,0:T(8,128)(2,1)} %copy-done.1, bf16[4,512,512]{2,1,0:T(8,128)(2,1)} %constant.42.clone.wide_from, bf16[4,512,512]{2,1,0:T(8,128)(2,1)} %constant.43.clone.tall_from), custom_call_target="tpu_custom_call" | custom-call | tf_op jit(solution)/shard_map/pallas_call | solution.py:291
  53.5 31.6 %all_to_all.16 = bf16[16,64,1024]{2,1,0:T(8,128)(2,1)S(1)} all-to-all(bf16[16,64,1024]{2,1,0:T(8,128)(2,1)} %bitcast.18), channel_id=1, replica_groups=mesh['chan'=8,'row'=16] {'row'}, dimensions={0} | all-to-all | bytes 4194304 | tf_op jit(solution)/shard_map/all_to_all | solution.py:357
  85.1 0.4 convert_reduce_fusion
  85.5 0.7 multiply_bitcast_fusion
  (6 shorter events, 0.1 us)
Async XLA Ops:
  0.0 1.6 %copy-start = (bf16[8,16,2,4096]{3,2,1,0:T(2,128)(2,1)S(1)}, bf16[8,16,2,4096]{3,2,1,0:T(2,128)(2,1)}, u32[]{:S(2)}) copy-start(bf16[8,16,2,4096]{3,2,1,0:T(2,128)(2,1)} %param.8) | copy-start | bytes 6291460
  2.5 10.5 %all-to-all-start = ((bf16[8,2,32,128]{3,2,1,0:T(8,128)(2,1)}), bf16[8,2,32,128]{3,2,1,0:T(8,128)(2,1)S(1)}, u32[]{:S(2)}, u32[]{:S(2)}) async-start(bf16[8,2,32,128]{3,2,1,0:T(8,128)(2,1)} %reshape.45), calls=%async_computation | async-start | bytes 262144 | tf_op jit(solution)/shard_map/all_to_all | solution.py:342
  13.0 19.2 %copy-start.2 = (bf16[8,2,32,128]{3,2,1,0:T(8,128)(2,1)}, bf16[8,2,32,128]{3,2,1,0:T(8,128)(2,1)S(1)}, u32[]{:S(2)}) copy-start(bf16[8,2,32,128]{3,2,1,0:T(8,128)(2,1)S(1)} %all-to-all-done.volts) | copy-start | bytes 393220
  30.8 1.4 %copy-start.1 = (s16[16,3,32,128]{3,2,1,0:T(8,128)(2,1)}, s16[16,3,32,128]{3,2,1,0:T(8,128)(2,1)S(1)}, u32[]{:S(2)}) copy-start(s16[16,3,32,128]{3,2,1,0:T(8,128)(2,1)S(1)} %all_to_all.15.lists) | copy-start | bytes 1179652
